TPU v7x, 32 devices: a whole 2x2x4 slice. The times are simulated.
32 devices in a mesh: img: 2 (over x), wide: 16 (over z, y, core).
Axes of the slice: x: 2, y: 2, z: 4, core: 2. Of those that a mesh axis runs over, the one named last changes fastest.
Arguments:
- latent: bfloat16 [64, 256, 320], P('img', 'wide'), parts along dimension 0, may hold values from -45 to 45
- group_norm_gain: float32 [320], replicated, may hold values from 0.25 to 1.75
- group_norm_shift: float32 [320], replicated, may hold values from -1.5 to 1.5
- kernel_weight: bfloat16 [3, 3, 320, 320], replicated, may hold values from -0.109375 to 0.109375
- kernel_bias: float32 [320], replicated, may hold values from -0.8 to 0.8
Outputs:
- mixed: bfloat16 [64, 256, 320], P('img', 'wide'), parts along dimension 0
There are 2 independent parts, one for each index of `img`. A program takes and returns all parts, laid end to end along the dimension named above; an argument that names none is the same for every part. Nothing has to cross between parts.
All inputs are finite; a program needn't handle non-finite values.
Results may differ from a plain program's by a relative error of at most 0.0085.
Values may be sent and summed in bfloat16 or wider, within the bound.
No kernel may reach another device: no remote copies, remote signals or barrier semaphores. Data moves between devices by JAX's collectives and lax.ppermute only.
A program may use at most 64 MiB of HBM per device.

v0:
```python
import jax
import jax.numpy as jnp
from jax import lax
from jax.sharding import PartitionSpec as P

NORM_GROUPS = 32
TILE = 128
OVER = 32
DILATION_FACTOR = 8
STRIDE = 96


epsilon = 1e-05


def with_halo(cells, sides, width):
    for axis, dim in sides:
        count = lax.axis_size(axis)
        ends = count - 1
        head = lax.slice_in_dim(cells, 0, width, axis=dim)
        tail = lax.slice_in_dim(cells, cells.shape[dim] - width, cells.shape[dim], axis=dim)
        cells = jnp.concatenate(
            [
                lax.ppermute(tail, axis, [(i, (i + 1) % count) for i in range(ends)]),
                cells,
                lax.ppermute(head, axis, [((i + 1) % count, i) for i in range(ends)]),
            ],
            axis=dim,
        )
    return cells


def group_normalize(value_array, mean_value, inverse, group_norm_gain, group_norm_shift):
    return jax.nn.silu((value_array - mean_value) * inverse * group_norm_gain + group_norm_shift)


def group_inverse(running, squares, entry_items):
    mean_group = running / entry_items
    inverse = lax.rsqrt(squares / entry_items - mean_group * mean_group + epsilon)
    return (mean_group, inverse)


def convolve_taps(sources, kernel_weight, kernel_bias, spacing):
    leading = sources[0].shape[:-2]
    width_out = sources[0].shape[-2] - 2 * spacing
    channel_in = sources[0].shape[-1]
    running = None
    for kernel_row in range(3):
        for kernel_col in range(3):
            sliced = sources[kernel_row][
                ..., kernel_col * spacing : kernel_col * spacing + width_out, :
            ]
            sliced = sliced.reshape(-1, channel_in)
            term = jnp.dot(
                sliced, kernel_weight[kernel_row, kernel_col], preferred_element_type=jnp.float32
            )
            running = term if running is None else running + term
    shaped = running.reshape(leading + (width_out, kernel_weight.shape[3]))
    return (shaped + kernel_bias).astype(jnp.bfloat16)


def local_path(latent, group_norm_gain, group_norm_shift, kernel_weight, kernel_bias):
    device_index = lax.axis_index("wide")
    device_count = lax.axis_size("wide")
    row_total, column_total, channel_total = latent.shape
    half_over = OVER // 2
    channels_per_group = channel_total // NORM_GROUPS
    blocks_stride = STRIDE // column_total
    rim_blocks = half_over // column_total
    tile_blocks = TILE // column_total
    value_array = latent.astype(jnp.float32).reshape(
        row_total, column_total, NORM_GROUPS, channels_per_group
    )
    own_sum = jnp.sum(value_array, axis=(0, 1, 3))
    own_squares = jnp.sum(value_array * value_array, axis=(0, 1, 3))
    all_sums, all_squares = (
        lax.all_gather(own_sum[None], "wide", axis=0, tiled=True),
        lax.all_gather(own_squares[None], "wide", axis=0, tiled=True),
    )
    first_tile = (device_index + rim_blocks) // blocks_stride
    tile_ids = jnp.stack([first_tile, first_tile - 1])
    start_blocks = tile_ids * blocks_stride - rim_blocks
    block_ids = jnp.arange(device_count, dtype=jnp.int32)
    select = (
        (block_ids[None, :] >= start_blocks[:, None])
        & (block_ids[None, :] < start_blocks[:, None] + tile_blocks)
    ).astype(jnp.float32)
    running = jnp.dot(select, all_sums, precision=lax.Precision.HIGHEST)
    squares = jnp.dot(select, all_squares, precision=lax.Precision.HIGHEST)
    entry_items = (jnp.sum(select, axis=1) * (row_total * column_total * channels_per_group))[
        :, None
    ]
    mean_group, inverse = group_inverse(running, squares, entry_items)
    channel_mean = jnp.repeat(mean_group, channels_per_group, axis=1)[:, None, None, :]
    channel_inverse_scale = jnp.repeat(inverse, channels_per_group, axis=1)[:, None, None, :]
    widened = with_halo(latent, (("wide", 1),), 1)
    columns = device_index * column_total - 1 + jnp.arange(column_total + 2, dtype=jnp.int32)
    tile_start = tile_ids * STRIDE - half_over
    inside = (columns[None, :] >= tile_start[:, None]) & (
        columns[None, :] < tile_start[:, None] + TILE
    )
    inside = (
        inside & (columns[None, :] >= 0) & (columns[None, :] < device_count * column_total)
    ).astype(jnp.float32)
    apply_silu = group_normalize(
        widened.astype(jnp.float32)[None],
        channel_mean,
        channel_inverse_scale,
        group_norm_gain,
        group_norm_shift,
    )
    apply_silu = (apply_silu * inside[:, None, :, None]).astype(jnp.bfloat16)
    padded = jnp.pad(apply_silu, ((0, 0), (1, 1), (0, 0), (0, 0)))
    tile_out = convolve_taps(
        (padded[:, 0:row_total], padded[:, 1 : row_total + 1], padded[:, 2 : row_total + 2]),
        kernel_weight,
        kernel_bias,
        1,
    )
    own_cols = device_index * column_total + jnp.arange(column_total, dtype=jnp.int32)
    offset = own_cols[None, :] - tile_start[:, None]
    covered = ((offset >= 0) & (offset < TILE) & (tile_ids[:, None] >= 0)).astype(jnp.float32)
    offset_float = offset.astype(jnp.float32)
    ramp = jnp.minimum(offset_float + 1.0, TILE - offset_float) * covered
    numer = jnp.sum(ramp[:, None, :, None] * tile_out.astype(jnp.float32), axis=0)
    return numer / jnp.sum(ramp, axis=0)[None, :, None]


def dilated_path(latent, group_norm_gain, group_norm_shift, kernel_weight, kernel_bias):
    device_count = lax.axis_size("wide")
    row_total, column_total, channel_total = latent.shape
    channels_per_group = channel_total // NORM_GROUPS
    sublatent_height = row_total // DILATION_FACTOR
    sublatent_columns = column_total // DILATION_FACTOR
    value_array = latent.astype(jnp.float32).reshape(
        sublatent_height,
        DILATION_FACTOR,
        sublatent_columns,
        DILATION_FACTOR,
        NORM_GROUPS,
        channels_per_group,
    )
    totals = lax.psum(
        (jnp.sum(value_array, axis=(0, 2, 5)), jnp.sum(value_array * value_array, axis=(0, 2, 5))),
        "wide",
    )
    entry_items = sublatent_height * (sublatent_columns * device_count) * channels_per_group
    mean_group, inverse = group_inverse(totals[0], totals[1], entry_items)
    channel_mean = jnp.repeat(mean_group, channels_per_group, axis=2)[None, :, None, :, :]
    channel_inverse_scale = jnp.repeat(inverse, channels_per_group, axis=2)[None, :, None, :, :]
    apply_silu = group_normalize(
        value_array.reshape(
            sublatent_height, DILATION_FACTOR, sublatent_columns, DILATION_FACTOR, channel_total
        ),
        channel_mean,
        channel_inverse_scale,
        group_norm_gain,
        group_norm_shift,
    )
    apply_silu = apply_silu.astype(jnp.bfloat16).reshape(row_total, column_total, channel_total)
    arrived = with_halo(apply_silu, (("wide", 1),), DILATION_FACTOR)
    widened = jnp.pad(arrived, ((DILATION_FACTOR, DILATION_FACTOR), (0, 0), (0, 0)))
    sources = (
        widened[0:row_total],
        widened[DILATION_FACTOR : DILATION_FACTOR + row_total],
        widened[2 * DILATION_FACTOR : 2 * DILATION_FACTOR + row_total],
    )
    return convolve_taps(sources, kernel_weight, kernel_bias, DILATION_FACTOR)


def local(latent, group_norm_gain, group_norm_shift, kernel_weight, kernel_bias):
    blended = local_path(latent, group_norm_gain, group_norm_shift, kernel_weight, kernel_bias)
    global_out = dilated_path(latent, group_norm_gain, group_norm_shift, kernel_weight, kernel_bias)
    return (0.5 * (blended + global_out.astype(jnp.float32))).astype(jnp.bfloat16)


def solution(mesh):
    in_specs = (P("img", "wide", None), P(), P(), P(), P())
    out_specs = P("img", "wide", None)
    return jax.shard_map(local, mesh=mesh, in_specs=in_specs, out_specs=out_specs, check_vma=False)
```

profile of v0, /device:TPU:0, one launch (start us, length us, event | category | flops | bytes accessed | tf_op | source)
XLA Modules:
  0.0 124.2 jit_solution(18425457740581956449)
XLA Ops:
  0.0 1.1 fusion.58
  1.1 1.3 %collective-permute-start.1 = (bf16[32,1,320]{2,1,0:T(2,128)(2,1)S(1)}, bf16[32,1,320]{2,1,0:T(2,128)(2,1)S(1)}, u32[]{:S(2)}, u32[]{:S(2)}) collective-permute-start(bf16[32,1,320]{2,1,0:T(2,128)(2,1)S(1)} %get-tuple-element.37), channel_id=1, source_target_pairs={{1,0},{2,1},{3,2},{4,3},{5,4},{6,5},{7,6},{8,7},{9,8},{10,9},{11,1... | collective-permute-start | bytes 61448 | tf_op jit(solution)/shard_map/ppermute | solution.py:26
  2.4 3.0 %collective-permute-start = (bf16[32,1,320]{2,1,0:T(2,128)(2,1)S(1)}, bf16[32,1,320]{2,1,0:T(2,128)(2,1)S(1)}, u32[]{:S(2)}, u32[]{:S(2)}) collective-permute-start(bf16[32,1,320]{2,1,0:T(2,128)(2,1)S(1)} %get-tuple-element.36), channel_id=1, source_target_pairs={{0,1},{1,2},{2,3},{3,4},{4,5},{5,6},{6,7},{7,8},{8,9},{9,10},{10,1... | collective-permute-start | bytes 61448 | tf_op jit(solution)/shard_map/ppermute | solution.py:24
  5.4 1.1 convert_reduce_fusion
  6.6 11.1 %reshape.391 = f32[4,8,2,8,32,10]{5,4,3,2,1,0:T(8,128)} reshape(bf16[32,16,320]{2,1,0:T(8,128)(2,1)} %param.5) | data formatting | bytes 983040 | tf_op jit(solution)/shard_map/reshape | solution.py:135
  17.7 0.1 reduce_sum.82
  17.8 0.1 reduce_sum.78
  17.9 5.1 %fusion.54 = (f32[8,8,32]{2,1,0:T(8,128)S(1)}, f32[8,8,32]{2,1,0:T(8,128)S(1)}) fusion(f32[4,8,2,8,32,10]{5,4,3,2,1,0:T(8,128)} %reshape.391), kind=kLoop, calls=%fused_computation.109 | loop fusion | flops 487424 | bytes 671744 | tf_op jit(solution)/shard_map/reduce_sum | solution.py:144
  23.0 0.1 reduce_sum.83
  23.2 0.6 dynamic-slice
  24.4 0.1 reduce_sum.79
  24.5 0.2 dynamic-update-slice.1
  24.8 0.2 dynamic-update-slice
  25.0 63.3 %all-reduce.4 = (f32[512]{0:T(512)S(1)}, f32[512]{0:T(512)S(1)}, f32[8,8,32]{2,1,0:T(8,128)S(1)}, f32[8,8,32]{2,1,0:T(8,128)S(1)}) all-reduce(f32[512]{0:T(512)S(1)} %dynamic-update-slice.1, f32[512]{0:T(512)S(1)} %dynamic-update-slice, f32[8,8,32]{2,1,0:T(8,128)S(1)} %get-tuple-element.6, ...), channel_id=3, replica_groups=mesh['img'=2,'wide'=16] {'wide'}, use_global_device_ids=true, to_apply=%add.3 | all-reduce | flops 5120 | bytes 40960
  88.3 0.3 broadcast_in_dim.17
  88.6 0.6 mul.169
  89.2 0.3 broadcast_in_dim.16
  89.6 0.6 sub.102
  90.4 0.2 copy-done
  90.6 0.3 multiply_convert_fusion.3
  90.9 0.8 fusion.57
  91.6 1.4 %collective-permute-start.3 = (bf16[32,8,320]{2,1,0:T(8,128)(2,1)}, bf16[32,8,320]{2,1,0:T(8,128)(2,1)}, u32[]{:S(2)}, u32[]{:S(2)}) collective-permute-start(bf16[32,8,320]{2,1,0:T(8,128)(2,1)} %get-tuple-element.35), channel_id=1, source_target_pairs={{1,0},{2,1},{3,2},{4,3},{5,4},{6,5},{7,6},{8,7},{9,8},{10,9},{11,1... | collective-permute-start | bytes 491528 | tf_op jit(solution)/shard_map/ppermute | solution.py:26
  93.1 3.7 %collective-permute-start.2 = (bf16[32,8,320]{2,1,0:T(8,128)(2,1)}, bf16[32,8,320]{2,1,0:T(8,128)(2,1)}, u32[]{:S(2)}, u32[]{:S(2)}) collective-permute-start(bf16[32,8,320]{2,1,0:T(8,128)(2,1)} %get-tuple-element.34), channel_id=1, source_target_pairs={{0,1},{1,2},{2,3},{3,4},{4,5},{5,6},{6,7},{7,8},{8,9},{9,10},{10,1... | collective-permute-start | bytes 491528 | tf_op jit(solution)/shard_map/ppermute | solution.py:24
  96.8 0.9 convert_element_type.69
  97.7 0.1 broadcast_compare_fusion.2
  97.8 0.1 reshape.402
  97.9 0.1 reshape.401
  98.0 0.2 convert_reduce_fusion.1
  98.2 1.4 %multiply_convert_fusion.2 = bf16[4,8,2,8,320]{4,3,2,1,0:T(8,128)(2,1)S(1)} fusion(f32[4,8,2,8,320]{4,3,2,1,0:T(8,128)} %bitcast.97, f32[320]{0:T(512)S(1)} %copy-done.3, f32[320]{0:T(512)S(1)} %copy-done.4, f32[8,8,320]{2,1,0:T(8,128)S(1)} %mul.169, f32[8,8,320]{2,1,0:T(8,128)S(1)} %sub.102), kind=kLoop, calls=%fused_computation.35 | loop fusion | flops 1474560 | bytes 1149440 | tf_op jit(solution)/shard_map/convert_element_type | solution.py:160
  99.6 0.2 convolution_divide_fusion.1
  99.8 0.2 fusion.10
  100.0 1.2 %fusion.20 = f32[512,320]{0,1:T(8,128)} fusion(bf16[512,320]{1,0:T(8,128)(2,1)S(1)} %bitcast.116, bf16[3,3,320,320]{3,2,1,0:T(8,128)(2,1)S(1)} %copy-done.1), kind=kOutput, calls=%fused_computation.57 | convolution fusion | flops 104857600 | bytes 1294336 | tf_op jit(solution)/shard_map/dot_general | solution.py:54
  101.2 0.1 and_convert_fusion
  101.3 0.1 fusion.55
  101.4 0.1 mul.158
  101.6 0.1 broadcast_in_dim.13
  101.6 0.1 sub.97
  101.8 0.3 maximum_convert_fusion
  102.0 0.8 multiply_convert_fusion
  102.9 1.6 %pad_slice_fusion = (bf16[2,32,16,320]{3,2,1,0:T(8,128)(2,1)S(1)}, bf16[2,32,16,320]{3,2,1,0:T(8,128)(2,1)S(1)}, bf16[2,32,16,320]{3,2,1,0:T(8,128)(2,1)S(1)}, b...) fusion(bf16[2,32,18,320]{3,2,1,0:T(8,128)(2,1)S(1)} %multiply_c, ...), kind=kLoop, calls=%fused_computation.38 | loop fusion | bytes 9437184 | tf_op jit(solution)/shard_map/slice | solution.py:50
  104.5 0.6 fusion.31
  105.1 0.6 convolution_add_fusion.7
  105.7 0.6 convolution_add_fusion.6
  106.2 0.6 convolution_add_fusion.5
  106.8 0.6 convolution_add_fusion.4
  107.3 0.6 convolution_add_fusion.3
  107.9 0.6 convolution_add_fusion.2
  108.5 0.6 convolution_add_fusion.1
  109.0 1.6 %convolution_add_fusion = f32[1024,320]{0,1:T(8,128)} fusion(f32[1024,320]{0,1:T(8,128)S(1)} %convolution_add_fusion.1, bf16[1024,320]{1,0:T(8,128)(2,1)S(1)} %bitcast.100, bf16[3,3,320,320]{3,2,1,0:T(8,128)(2,1)S(1)} %copy-done.1), kind=kOutput, calls=%fused_computation.7 | convolution fusion | flops 210042880 | bytes 3653632 | tf_op jit(solution)/shard_map/dot_general | solution.py:54
  110.7 3.0 %copy.9 = f32[1024,320]{1,0:T(8,128)} copy(f32[1024,320]{0,1:T(8,128)} %convolution_add_fusion) | data formatting | bytes 2621440 | tf_op jit(solution)/shard_map/add | solution.py:57
  113.6 1.7 %multiply_reduce_fusion.1 = f32[32,16,320]{2,1,0:T(8,128)S(1)} fusion(f32[2,32,16,320]{3,2,1,0:T(8,128)} %bitcast.95, f32[320]{0:T(512)S(1)} %copy-done.5, f32[2,16]{1,0:T(2,128)S(1)} %get-tuple-element.14), kind=kLoop, calls=%fused_computation.5 | loop fusion | flops 1474560 | bytes 1967488 | tf_op jit(solution)/shard_map/reduce_sum | solution.py:125
  115.4 1.1 fusion.7
  116.5 0.2 fusion.56
  116.8 0.4 fusion.15
  117.2 0.4 fusion.29
  117.6 0.4 convolution_add_fusion.13
  118.0 0.4 convolution_add_fusion.12
  118.4 1.1 pad_maximum_fusion
  119.5 0.4 fusion.5
  119.9 0.4 fusion.4
  120.3 0.4 convolution_add_fusion.9
  120.7 1.2 convolution_add_fusion.8
  121.9 1.3 %copy.10 = f32[512,320]{1,0:T(8,128)S(1)} copy(f32[512,320]{0,1:T(8,128)} %convolution_add_fusion.8) | data formatting | bytes 1310720 | tf_op jit(solution)/shard_map/add | solution.py:57
  123.2 0.9 multiply_convert_fusion.1
  (28 shorter events, 0.3 us)
Async XLA Ops:
  1.1 100.6 %collective-permute-start.1 = (bf16[32,1,320]{2,1,0:T(2,128)(2,1)S(1)}, bf16[32,1,320]{2,1,0:T(2,128)(2,1)S(1)}, u32[]{:S(2)}, u32[]{:S(2)}) collective-permute-start(bf16[32,1,320]{2,1,0:T(2,128)(2,1)S(1)} %get-tuple-element.37), channel_id=1, source_target_pairs={{1,0},{2,1},{3,2},{4,3},{5,4},{6,5},{7,6},{8,7},{9,8},{10,9},{11,1... | collective-permute-start | bytes 61448 | tf_op jit(solution)/shard_map/ppermute | solution.py:26
  2.4 99.4 %collective-permute-start = (bf16[32,1,320]{2,1,0:T(2,128)(2,1)S(1)}, bf16[32,1,320]{2,1,0:T(2,128)(2,1)S(1)}, u32[]{:S(2)}, u32[]{:S(2)}) collective-permute-start(bf16[32,1,320]{2,1,0:T(2,128)(2,1)S(1)} %get-tuple-element.36), channel_id=1, source_target_pairs={{0,1},{1,2},{2,3},{3,4},{4,5},{5,6},{6,7},{7,8},{8,9},{9,10},{10,1... | collective-permute-start | bytes 61448 | tf_op jit(solution)/shard_map/ppermute | solution.py:24
  17.9 5.3 %copy-start.6 = (u32[32]{0:T(128)S(1)}, u32[32]{0:T(128)}, u32[]{:S(2)}) copy-start(u32[32]{0:T(128)} %constant.72) | copy-start | bytes 388
  89.6 1.0 copy-start
  89.6 1.0 copy-start.3
  89.6 1.0 copy-start.4
  91.6 8.3 %copy-start.1 = (bf16[3,3,320,320]{3,2,1,0:T(8,128)(2,1)S(1)}, bf16[3,3,320,320]{3,2,1,0:T(8,128)(2,1)}, u32[]{:S(2)}) copy-start(bf16[3,3,320,320]{3,2,1,0:T(8,128)(2,1)} %param.8) | copy-start | bytes 5529604
  91.6 23.7 %collective-permute-start.3 = (bf16[32,8,320]{2,1,0:T(8,128)(2,1)}, bf16[32,8,320]{2,1,0:T(8,128)(2,1)}, u32[]{:S(2)}, u32[]{:S(2)}) collective-permute-start(bf16[32,8,320]{2,1,0:T(8,128)(2,1)} %get-tuple-element.35), channel_id=1, source_target_pairs={{1,0},{2,1},{3,2},{4,3},{5,4},{6,5},{7,6},{8,7},{9,8},{10,9},{11,1... | collective-permute-start | bytes 491528 | tf_op jit(solution)/shard_map/ppermute | solution.py:26
  93.1 22.3 %collective-permute-start.2 = (bf16[32,8,320]{2,1,0:T(8,128)(2,1)}, bf16[32,8,320]{2,1,0:T(8,128)(2,1)}, u32[]{:S(2)}, u32[]{:S(2)}) collective-permute-start(bf16[32,8,320]{2,1,0:T(8,128)(2,1)} %get-tuple-element.34), channel_id=1, source_target_pairs={{0,1},{1,2},{2,3},{3,4},{4,5},{5,6},{6,7},{7,8},{8,9},{9,10},{10,1... | collective-permute-start | bytes 491528 | tf_op jit(solution)/shard_map/ppermute | solution.py:24
  110.7 3.0 %copy-start.5 = (f32[320]{0:T(512)S(1)}, f32[320]{0:T(512)}, u32[]{:S(2)}) copy-start(f32[320]{0:T(512)} %param.9) | copy-start | bytes 3844
  118.0 1.5 %copy-start.2 = (f32[512,320]{0,1:T(8,128)S(1)}, f32[512,320]{0,1:T(8,128)}, u32[]{:S(2)}) copy-start(f32[512,320]{0,1:T(8,128)} %fusion.20) | copy-start | bytes 1966084
where the time goes:
time: 125 us; the launch traced here: 124 us
  blocking collectives  63.3 us (51%)
  local copies, waits for them, and re-layouts  23.2 us (19%)
  other arithmetic  15.6 us (12%)
  matrix products  11.6 us (9%)
  starting transfers between devices  9.45 us (8%)
    unnamed x1, blocking collectives  63.3 us
    dot_general x18, matrix products, convolve_taps(): jnp.dot(sliced, kernel_weight[kernel_row, kernel_col], preferred_element_...  11.2 us
    reshape x1, local copies, waits for them, and re-layouts, dilated_path(): latent.astype(jnp.float32)  11.1 us
    ppermute x2, starting transfers between devices, with_halo(): lax.ppermute(tail, axis, [(i, (i + 1) % count) for i in range(ends)])  6.75 us
    reduce_sum x1, other arithmetic, dilated_path(): jnp.sum(value_array, axis=(0, 2, 5))  5.12 us
    add x2, local copies, waits for them, and re-layouts, convolve_taps(): running = term if running is None else running + term  4.3 us
    ppermute x2, starting transfers between devices, with_halo(): lax.ppermute(head, axis, [((i + 1) % count, i) for i in range(ends)])  2.7 us
  transfers between devices with their start and end apart: 4, of which 0 were waited for; matrix products, arithmetic and copies ran while one was open for 32% of the time, Pallas kernels for 0%

commit v1 on v0

v1 whole, which is shorter than its diff:
```python
import jax
import jax.numpy as jnp
from jax import lax
from jax.experimental import pallas as pl
from jax.experimental.pallas import tpu as pltpu
from jax.sharding import PartitionSpec as P

NORM_GROUPS = 32
TILE = 128
OVER = 32
DIL = 8
STRIDE = 96
EPS = 1e-05
F32 = jnp.float32
BF16 = jnp.bfloat16


def iota(shape, dim):
    return lax.broadcasted_iota(jnp.int32, shape, dim)


def group_onehot(channels, per_group, offset):
    lane = iota((128, channels), 0) - offset
    first = lane * per_group
    ch = iota((128, channels), 1)
    return ((ch >= first) & (ch < first + per_group) & (lane >= 0)).astype(F32)


def group_onehot_t(channels, per_group, offset):
    lane = iota((channels, 128), 1) - offset
    first = lane * per_group
    ch = iota((channels, 128), 0)
    return ((ch >= first) & (ch < first + per_group) & (lane >= 0)).astype(F32)


def make_stats(rows, cols, channels, tile_rows):
    per_group = channels // NORM_GROUPS
    rim_blocks = (OVER // 2) // cols
    stride_blocks = STRIDE // cols
    tile_blocks = TILE // cols

    def kernel(x_ref, stats_ref, ea_ref, eb_ref, s_ref, q_ref):
        block = lax.axis_index("wide")
        even = lax.rem(block, 2) == 0
        for a in range(0, DIL, 2):
            s = [jnp.zeros((8, channels), F32) for _ in range(2)]
            q = [jnp.zeros((8, channels), F32) for _ in range(2)]
            for rr in range(rows // DIL):
                pa, pb = [], []
                for u in range(2):
                    r = rr * DIL + a + u
                    x = x_ref[r * cols : (r + 1) * cols, :].astype(F32)
                    lo, hi = x[:8], x[8:]
                    s[u] += lo + hi
                    q[u] += lo * lo + hi * hi
                    pa.append(jnp.where(even, hi, lo))
                    pb.append(jnp.where(even, lo, hi))
                r0 = (rr * DIL + a) * 8
                ea_ref[r0 : r0 + 16, :] = jnp.concatenate(pa, axis=0).astype(BF16)
                eb_ref[r0 : r0 + 16, :] = jnp.concatenate(pb, axis=0).astype(BF16)
            for u in range(2):
                s_ref[(a + u) * 8 : (a + u) * 8 + 8, :] = s[u]
                q_ref[(a + u) * 8 : (a + u) * 8 + 8, :] = q[u]
        total = None
        for ref, half, offset in (
            (s_ref, 0, 0),
            (s_ref, 1, 32),
            (q_ref, 0, 64),
            (q_ref, 1, 96),
        ):
            term = jnp.dot(
                ref[half * 32 : half * 32 + 32, :],
                group_onehot_t(channels, per_group, offset),
                precision=lax.Precision.HIGHEST,
                preferred_element_type=F32,
            )
            total = term if total is None else total + term
        stats_ref[0:32, :] = total
        line = jnp.sum(total, axis=0, keepdims=True)
        line = jnp.broadcast_to(line, (8, 128))
        line = line + pltpu.roll(line, 96, 1)
        for k in range(tile_rows // 8):
            start = (iota((8, 128), 0) + 8 * k) * stride_blocks - rim_blocks
            covers = (block >= start) & (block < start + tile_blocks)
            stats_ref[32 + 8 * k : 40 + 8 * k, :] = jnp.where(covers, line, 0.0)

    return pl.pallas_call(
        kernel,
        out_shape=(
            jax.ShapeDtypeStruct((32 + tile_rows, 128), F32),
            jax.ShapeDtypeStruct((rows * 8, channels), BF16),
            jax.ShapeDtypeStruct((rows * 8, channels), BF16),
        ),
        scratch_shapes=[
            pltpu.VMEM((64, channels), F32),
            pltpu.VMEM((64, channels), F32),
        ],
        compiler_params=pltpu.CompilerParams(vmem_limit_bytes=16 * 2**20),
        name="block_stats",
    )


def make_main(rows, cols, channels, out_channels, tile_rows, count):
    per_group = channels // NORM_GROUPS
    rim = OVER // 2
    rim_blocks = rim // cols
    stride_blocks = STRIDE // cols
    tile_blocks = TILE // cols
    pixels = rows * cols
    main = (channels // 128) * 128
    rem = channels - main
    depth = 9 * channels
    sub_items = float((rows // DIL) * (cols // DIL) * count * per_group)
    all_rows = 32 + tile_rows

    def kernel(
        x_ref, ha_ref, hb_ref, stats_ref, gain_ref, shift_ref, bias_ref, w_hbm, o_ref,
        w_ref, a_ref, sub_ref, blend_ref, sc_ref, sh_ref, tsc_ref, tsh_ref, bw_ref, sem,
    ):
        copies = []
        for tap in range(9):
            i, j = tap // 3, tap % 3
            copies.append(
                pltpu.make_async_copy(
                    w_hbm.at[i, j, pl.ds(0, main), :],
                    w_ref.at[pl.ds(tap * main, main), :],
                    sem.at[2 * tap],
                )
            )
            copies.append(
                pltpu.make_async_copy(
                    w_hbm.at[i, j, pl.ds(main, rem), :],
                    w_ref.at[pl.ds(9 * main + tap * rem, rem), :],
                    sem.at[2 * tap + 1],
                )
            )
        for c in copies:
            c.start()

        block = lax.axis_index("wide")
        even = lax.rem(block, 2) == 0
        tile0 = lax.div(block + rim_blocks, stride_blocks)
        tile1 = tile0 - 1

        stats = stats_ref[...]
        row_id = iota((all_rows, 128), 0)
        lane_id = iota((all_rows, 128), 1)
        start = (row_id - 32) * stride_blocks - rim_blocks
        blocks = jnp.minimum(start + tile_blocks, count) - jnp.maximum(start, 0)
        tile_items = jnp.maximum(blocks, 1).astype(F32) * float(pixels * per_group)
        is_sub = row_id < 32
        items = jnp.where(is_sub, sub_items, tile_items)
        mean = stats / items
        square = pltpu.roll(stats, 64, 1) / items
        inverse = lax.rsqrt(square - mean * mean + EPS)
        valid = lane_id < jnp.where(is_sub, 64, 32)
        mean = jnp.where(valid, mean, 0.0)
        inverse = jnp.where(valid, inverse, 0.0)
        both = jnp.concatenate([mean, inverse], axis=0)
        gain = 0.5 * gain_ref[...]
        shift = 0.5 * shift_ref[...]
        for half in range(2):
            wide = jnp.dot(
                both,
                group_onehot(channels, per_group, 32 * half),
                precision=lax.Precision.HIGHEST,
                preferred_element_type=F32,
            )
            scale = wide[all_rows:] * gain
            offset = shift - wide[:all_rows] * scale
            sc_ref[32 * half : 32 * half + 32, :] = scale[:32]
            sh_ref[32 * half : 32 * half + 32, :] = offset[:32]
            if half == 0:
                tile_row = iota((tile_rows, channels), 0)
                for t, tid in enumerate((tile0, tile1)):
                    pick = tile_row == jnp.maximum(tid, 0)
                    for ref, values in ((tsc_ref, scale), (tsh_ref, offset)):
                        line = jnp.sum(
                            jnp.where(pick, values[32:], 0.0), axis=0, keepdims=True
                        )
                        ref[8 * t : 8 * t + 8, :] = jnp.broadcast_to(line, (8, channels))

        sub_id = iota((8, channels), 0)
        for k in range(3):
            if k < 2:
                col = sub_id + 8 * k
            else:
                col = jnp.where(sub_id < 4, sub_id + cols, sub_id - 8)
            col = col + block * cols
            in_image = (col >= 0) & (col < count * cols)
            for j in range(3):
                out_col = col - (j - 1)
                ramps = []
                for tid in (tile0, tile1):
                    q = out_col - (tid * STRIDE - rim)
                    ok = (q >= 0) & (q < TILE) & (tid >= 0)
                    ramp = jnp.minimum(q + 1, TILE - q).astype(F32)
                    ramps.append(jnp.where(ok, ramp, 0.0))
                whole = jnp.maximum(ramps[0] + ramps[1], 1.0)
                for t, tid in enumerate((tile0, tile1)):
                    q = col - (tid * STRIDE - rim)
                    ok = (q >= 0) & (q < TILE) & in_image
                    bw_ref[j, k, t] = jnp.where(ok, ramps[t] / whole, 0.0)

        left_ok = jnp.where(block > 0, 1.0, 0.0).astype(F32)
        right_ok = jnp.where(block < count - 1, 1.0, 0.0).astype(F32)

        for r in range(DIL):
            sub_ref[r] = jnp.zeros((4 * 8, channels), F32)
            sub_ref[rows + DIL + r] = jnp.zeros((4 * 8, channels), F32)
        for j in range(3):
            blend_ref[j, 0] = jnp.zeros((cols, channels), F32)
            blend_ref[j, rows + 1] = jnp.zeros((cols, channels), F32)

        def silu(x, scale, offset):
            h = x * scale + offset
            return h + h * jnp.tanh(h)

        def activate(m, carry):
            ha = ha_ref[pl.ds(pl.multiple_of(16 * m, 16), 16), :].astype(F32)
            hb = hb_ref[pl.ds(pl.multiple_of(16 * m, 16), 16), :].astype(F32)
            left = jnp.where(even, hb, ha)
            right = jnp.where(even, ha, hb)
            for u in range(2):
                r = 2 * m + u
                x = x_ref[pl.ds(pl.multiple_of(r * cols, cols), cols), :].astype(F32)
                xl, xr = left[8 * u : 8 * u + 8], right[8 * u : 8 * u + 8]
                x0, x1 = x[:8], x[8:]
                res = pl.multiple_of(lax.rem(r, DIL) * 8, 8)
                scale = sc_ref[pl.ds(res, 8), :]
                offset = sh_ref[pl.ds(res, 8), :]
                sub_ref[r + DIL, 0:8, :] = silu(xl, scale, offset) * left_ok
                sub_ref[r + DIL, 8:16, :] = silu(x0, scale, offset)
                sub_ref[r + DIL, 16:24, :] = silu(x1, scale, offset)
                sub_ref[r + DIL, 24:32, :] = silu(xr, scale, offset) * right_ok
                xh = jnp.where(sub_id < 4, xr, xl)
                acts = [
                    [silu(v, tsc_ref[8 * t : 8 * t + 8, :], tsh_ref[8 * t : 8 * t + 8, :]) for t in range(2)]
                    for v in (x0, x1, xh)
                ]

                def mix(j, k):
                    return bw_ref[j, k, 0] * acts[k][0] + bw_ref[j, k, 1] * acts[k][1]

                blend_ref[1, r + 1, 0:8, :] = mix(1, 0)
                blend_ref[1, r + 1, 8:16, :] = mix(1, 1)
                f = [pltpu.roll(mix(2, k), 7, 0) for k in range(3)]
                blend_ref[2, r + 1, 0:8, :] = jnp.where(sub_id < 7, f[0], f[1])
                blend_ref[2, r + 1, 8:16, :] = jnp.where(sub_id < 7, f[1], f[2])
                g = [pltpu.roll(mix(0, k), 1, 0) for k in range(3)]
                blend_ref[0, r + 1, 0:8, :] = jnp.where(sub_id > 0, g[0], g[2])
                blend_ref[0, r + 1, 8:16, :] = jnp.where(sub_id > 0, g[1], g[0])
            return carry

        lax.fori_loop(0, rows // 2, activate, 0)

        def gather(r, carry):
            at = pl.ds(pl.multiple_of(r * cols, cols), cols)
            held = None
            for tap in range(9):
                i, j = tap // 3, tap % 3
                v = (
                    blend_ref[j, r + i] + sub_ref[r + DIL * i, 8 * j : 8 * j + cols, :]
                ).astype(BF16)
                a_ref[at, tap * main : (tap + 1) * main] = v[:, :main]
                if rem:
                    base = 9 * main + tap * rem
                    if tap % 2 == 0 and tap < 8:
                        held = v[:, main:]
                    elif tap < 8:
                        a_ref[at, base - rem : base + rem] = jnp.concatenate(
                            [held, v[:, main:]], axis=1
                        )
                    else:
                        a_ref[at, base : base + rem] = v[:, main:]
            return carry

        lax.fori_loop(0, rows, gather, 0)
        for c in copies:
            c.wait()
        acc = jnp.dot(a_ref[...], w_ref[...], preferred_element_type=F32)
        o_ref[...] = (0.5 * acc + bias_ref[...]).astype(BF16)

    vmem = pl.BlockSpec(memory_space=pltpu.VMEM)
    return pl.pallas_call(
        kernel,
        in_specs=[vmem] * 7 + [pl.BlockSpec(memory_space=pl.ANY)],
        out_specs=vmem,
        out_shape=jax.ShapeDtypeStruct((pixels, out_channels), BF16),
        scratch_shapes=[
            pltpu.VMEM((depth, out_channels), BF16),
            pltpu.VMEM((pixels, depth), BF16),
            pltpu.VMEM((rows + 2 * DIL, 4 * 8, channels), F32),
            pltpu.VMEM((3, rows + 2, cols, channels), F32),
            pltpu.VMEM((64, channels), F32),
            pltpu.VMEM((64, channels), F32),
            pltpu.VMEM((16, channels), F32),
            pltpu.VMEM((16, channels), F32),
            pltpu.VMEM((3, 3, 2, 8, channels), F32),
            pltpu.SemaphoreType.DMA((18,)),
        ],
        compiler_params=pltpu.CompilerParams(vmem_limit_bytes=40 * 2**20),
        name="norm_conv",
    )


def make_local(count):
    def local(latent, gain, shift, weight, bias):
        rows, cols, channels = latent.shape
        out_channels = weight.shape[3]
        stride_blocks = STRIDE // cols
        tiles = -(-(count + (OVER // 2) // cols) // stride_blocks)
        tile_rows = -(-tiles // 8) * 8
        x = latent.reshape(rows * cols, channels)
        stats, edge_a, edge_b = make_stats(rows, cols, channels, tile_rows)(x)
        pairs_a = [(i, i ^ 1) for i in range(count)]
        pairs_b = []
        for i in range(1, count - 1, 2):
            pairs_b += [(i, i + 1), (i + 1, i)]
        halo_a = lax.ppermute(edge_a, "wide", pairs_a)
        halo_b = lax.ppermute(edge_b, "wide", pairs_b)
        step = 1
        while step < count:
            stats = stats + lax.ppermute(stats, "wide", [(i, i ^ step) for i in range(count)])
            step *= 2
        out = make_main(rows, cols, channels, out_channels, tile_rows, count)(
            x, halo_a, halo_b, stats, gain[None], shift[None], bias[None], weight
        )
        return out.reshape(rows, cols, out_channels)

    return local


def solution(mesh):
    in_specs = (P("img", "wide", None), P(), P(), P(), P())
    out_specs = P("img", "wide", None)
    return jax.shard_map(
        make_local(mesh.shape["wide"]),
        mesh=mesh,
        in_specs=in_specs,
        out_specs=out_specs,
        check_vma=False,
    )
```

time: 125 us -> 34.7 us (0.28)
  blocking collectives: 63.3 us -> 0 us
  local copies, waits for them, and re-layouts: 23.2 us -> 5.66 us
  other arithmetic: 15.6 us -> 0.02 us
  matrix products: 11.6 us -> 0 us
  Pallas kernels: 0 us -> 10.6 us
  waiting for transfers between devices: 0.01 us -> 4.87 us
  starting transfers between devices: 9.45 us -> 13.3 us
    unnamed x1 -> x0, blocking collectives: 63.3 us -> none
    dot_general x20 -> x0, matrix products: 11.6 us -> none  [the longest x18 11.2 us: convolve_taps(): jnp.dot(sliced, kernel_weight[kernel_row, kernel_col], preferred_element_...]
    reshape x1 -> x0, local copies, waits for them, and re-layouts: 11.1 us -> none  [dilated_path(): latent.astype(jnp.float32)]
    pallas_call x0 -> x2, Pallas kernels: none -> 10.6 us  [the longest x1 9.82 us: local(): make_main(rows, cols, channels, out_channels, tile_rows, count)]
    reduce_sum x7 -> x0, other arithmetic: 8.51 us -> none  [the longest x1 5.12 us: dilated_path(): jnp.sum(value_array, axis=(0, 2, 5))]
    ppermute x4 -> x6, waiting for transfers between devices: 0.01 us -> 4.87 us  [the longest x4 4.87 us: local(): lax.ppermute(stats, 'wide', [(i, i ^ step) for i in range(count)])]
    convert_element_type x7 -> x0, other arithmetic: 4.72 us -> none  [the longest x2 1.69 us: dilated_path(): apply_silu.astype(jnp.bfloat16)]
    add x2 -> x0, local copies, waits for them, and re-layouts: 4.3 us -> none  [convolve_taps(): running = term if running is None else running + term]
  transfers between devices with their start and end apart: 4 -> 6, of which waited for: 0 -> 3; matrix products, arithmetic and copies ran while one was open for 32% -> 6% of each run, Pallas kernels for 0% -> 0%
where the time goes in v1:
time: 34.7 us; the launch traced here: 34.4 us
  starting transfers between devices  13.3 us (38%)
  Pallas kernels  10.6 us (31%)
  local copies, waits for them, and re-layouts  5.66 us (16%)
  waiting for transfers between devices  4.87 us (14%)
    ppermute x4, starting transfers between devices, local(): lax.ppermute(stats, 'wide', [(i, i ^ step) for i in range(count)])  12.2 us
    pallas_call x1, Pallas kernels, local(): make_main(rows, cols, channels, out_channels, tile_rows, count)  9.82 us
    ppermute x4, waiting for transfers between devices, local(): lax.ppermute(stats, 'wide', [(i, i ^ step) for i in range(count)])  4.87 us
    unnamed x6, local copies, waits for them, and re-layouts  3.61 us
    pallas_call x1, Pallas kernels, local(): stats, edge_a, edge_b = make_stats(rows, cols, channels, tile_rows)(x)  0.74 us
  transfers between devices with their start and end apart: 6, of which 3 were waited for; matrix products, arithmetic and copies ran while one was open for 6% of the time, Pallas kernels for 0%

profile of v1, /device:TPU:0, one launch (start us, length us, event | category | flops | bytes accessed | tf_op | source)
XLA Modules:
  0.0 34.4 jit_solution(9289883132416583162)
XLA Ops:
  0.0 0.0 copy-start.1
  0.0 1.0 %copy-done.1 = bf16[32,16,320]{2,1,0:T(8,128)(2,1)S(1)} copy-done((bf16[32,16,320]{2,1,0:T(8,128)(2,1)S(1)}, bf16[32,16,320]{2,1,0:T(8,128)(2,1)}, u32[]{:S(2)}) %copy-start.1) | copy-done | bytes 327704
  1.0 0.7 %block_stats.1 = (f32[40,128]{1,0:T(8,128)S(1)}, bf16[256,320]{1,0:T(8,128)(2,1)S(1)}, bf16[256,320]{1,0:T(8,128)(2,1)S(1)}) custom-call(bf16[512,320]{1,0:T(8,128)(2,1)S(1)} %bitcast.2), custom_call_target="tpu_custom_call" | custom-call | tf_op jit(solution)/shard_map/block_stats/pallas_call | solution.py:315
  1.7 0.5 %collective-permute-start = (bf16[256,320]{1,0:T(8,128)(2,1)S(1)}, bf16[256,320]{1,0:T(8,128)(2,1)S(1)}, u32[]{:S(2)}, u32[]{:S(2)}) collective-permute-start(bf16[256,320]{1,0:T(8,128)(2,1)S(1)} %get-tuple-element.8), channel_id=1, source_target_pairs={{0,1},{1,0},{2,3},{3,2},{4,5},{5,4},{6,7},{7,6},{8,9},{9,8},{10,11... | collective-permute-start | bytes 491528 | tf_op jit(solution)/shard_map/ppermute | solution.py:320
  2.2 0.7 %collective-permute-start.1 = (bf16[256,320]{1,0:T(8,128)(2,1)S(1)}, bf16[256,320]{1,0:T(8,128)(2,1)S(1)}, u32[]{:S(2)}, u32[]{:S(2)}) collective-permute-start(bf16[256,320]{1,0:T(8,128)(2,1)S(1)} %get-tuple-element.9), channel_id=1, source_target_pairs={{1,2},{2,1},{3,4},{4,3},{5,6},{6,5},{7,8},{8,7},{9,10},{10,9},{11,... | collective-permute-start | bytes 491528 | tf_op jit(solution)/shard_map/ppermute | solution.py:321
  2.9 4.0 %collective-permute-start.2 = (f32[40,128]{1,0:T(8,128)S(1)}, f32[40,128]{1,0:T(8,128)S(1)}, u32[]{:S(2)}, u32[]{:S(2)}) collective-permute-start(f32[40,128]{1,0:T(8,128)S(1)} %get-tuple-element.10), channel_id=1, source_target_pairs={{0,1},{1,0},{2,3},{3,2},{4,5},{5,4},{6,7},{7,6},{8,9},{9,8},{10,11... | collective-permute-start | bytes 61448 | tf_op jit(solution)/shard_map/ppermute | solution.py:324
  6.8 0.8 %collective-permute-done.2 = f32[40,128]{1,0:T(8,128)S(1)} collective-permute-done((f32[40,128]{1,0:T(8,128)S(1)}, f32[40,128]{1,0:T(8,128)S(1)}, u32[]{:S(2)}, u32[]{:S(2)}) %collective-permute-start.2) | collective-permute-done | bytes 20512 | tf_op jit(solution)/shard_map/ppermute | solution.py:324
  7.7 1.5 %collective-permute-start.3 = (f32[40,128]{1,0:T(8,128)S(1)}, f32[40,128]{1,0:T(8,128)S(1)}, u32[]{:S(2)}, u32[]{:S(2)}) collective-permute-start(f32[40,128]{1,0:T(8,128)S(1)} %add.12), channel_id=1, source_target_pairs={{0,2},{1,3},{2,0},{3,1},{4,6},{5,7},{6,4},{7,5},{8,10},{9,11},{10,... | collective-permute-start | bytes 61448 | tf_op jit(solution)/shard_map/ppermute | solution.py:324
  9.2 2.3 %collective-permute-done.3 = f32[40,128]{1,0:T(8,128)S(1)} collective-permute-done((f32[40,128]{1,0:T(8,128)S(1)}, f32[40,128]{1,0:T(8,128)S(1)}, u32[]{:S(2)}, u32[]{:S(2)}) %collective-permute-start.3) | collective-permute-done | bytes 20512 | tf_op jit(solution)/shard_map/ppermute | solution.py:324
  11.5 3.5 %collective-permute-start.4 = (f32[40,128]{1,0:T(8,128)S(1)}, f32[40,128]{1,0:T(8,128)S(1)}, u32[]{:S(2)}, u32[]{:S(2)}) collective-permute-start(f32[40,128]{1,0:T(8,128)S(1)} %add.13), channel_id=1, source_target_pairs={{0,4},{1,5},{2,6},{3,7},{4,0},{5,1},{6,2},{7,3},{8,12},{9,13},{10,... | collective-permute-start | bytes 61448 | tf_op jit(solution)/shard_map/ppermute | solution.py:324
  15.0 1.8 %collective-permute-done.4 = f32[40,128]{1,0:T(8,128)S(1)} collective-permute-done((f32[40,128]{1,0:T(8,128)S(1)}, f32[40,128]{1,0:T(8,128)S(1)}, u32[]{:S(2)}, u32[]{:S(2)}) %collective-permute-start.4) | collective-permute-done | bytes 20512 | tf_op jit(solution)/shard_map/ppermute | solution.py:324
  16.7 3.2 %collective-permute-start.5 = (f32[40,128]{1,0:T(8,128)S(1)}, f32[40,128]{1,0:T(8,128)S(1)}, u32[]{:S(2)}, u32[]{:S(2)}) collective-permute-start(f32[40,128]{1,0:T(8,128)S(1)} %add.14), channel_id=1, source_target_pairs={{0,8},{1,9},{2,10},{3,11},{4,12},{5,13},{6,14},{7,15},{8,0},{9,1},... | collective-permute-start | bytes 61448 | tf_op jit(solution)/shard_map/ppermute | solution.py:324
  19.9 0.7 %broadcast_in_dim.9.gain_ref = f32[1,320]{1,0:T(1,128)S(1)} reshape(f32[320]{0:T(512)} %param.6) | data formatting | bytes 2560 | tf_op jit(solution)/shard_map/broadcast_in_dim | solution.py:327
  20.6 0.7 %broadcast_in_dim.10.shift_ref = f32[1,320]{1,0:T(1,128)S(1)} reshape(f32[320]{0:T(512)} %param.7) | data formatting | bytes 2560 | tf_op jit(solution)/shard_map/broadcast_in_dim | solution.py:327
  21.3 0.7 %broadcast_in_dim.11.bias_ref = f32[1,320]{1,0:T(1,128)S(1)} reshape(f32[320]{0:T(512)} %param.9) | data formatting | bytes 2560 | tf_op jit(solution)/shard_map/broadcast_in_dim | solution.py:327
  22.0 0.0 collective-permute-done.5
  22.0 0.0 collective-permute-done.ha_ref
  22.0 0.0 collective-permute-done.1.hb_ref
  22.0 0.0 copy-start
  22.0 1.6 %copy-done = bf16[3,3,320,320]{3,2,1,0:T(8,128)(2,1)S(1)} copy-done((bf16[3,3,320,320]{3,2,1,0:T(8,128)(2,1)S(1)}, bf16[3,3,320,320]{3,2,1,0:T(8,128)(2,1)}, u32[]{:S(2)}) %copy-start) | copy-done | bytes 1843224
  23.6 0.0 copy-start.2
  23.6 1.0 %copy-done.2 = bf16[32,16,320]{2,1,0:T(8,128)(2,1)S(1)} copy-done((bf16[32,16,320]{2,1,0:T(8,128)(2,1)S(1)}, bf16[32,16,320]{2,1,0:T(8,128)(2,1)}, u32[]{:S(2)}) %copy-start.2) | copy-done | bytes 327704
  24.6 9.8 %norm_conv.1 = bf16[512,320]{1,0:T(8,128)(2,1)} custom-call(bf16[512,320]{1,0:T(8,128)(2,1)S(1)} %bitcast.3, bf16[256,320]{1,0:T(8,128)(2,1)S(1)} %collective-permute-done.ha_ref, bf16[256,320]{1,0:T(8,128)(2,1)S(1)} %collective-permute-done.1.hb_ref, f32[40,128]{1,0:T(8,128)S(1)} %add.15.stats_ref, f32[1,320]{1,0:T(1,128)S(1)} %broadcast_in_dim.9.gain_ref, ...), custom_call_target="tpu_custom_call" | custom-call | tf_op jit(solution)/shard_map/norm_conv/pallas_call | solution.py:326
  (4 shorter events, 0.0 us)
Async XLA Ops:
  0.0 1.0 %copy-start.1 = (bf16[32,16,320]{2,1,0:T(8,128)(2,1)S(1)}, bf16[32,16,320]{2,1,0:T(8,128)(2,1)}, u32[]{:S(2)}) copy-start(bf16[32,16,320]{2,1,0:T(8,128)(2,1)} %param.5) | copy-start | bytes 983044
  1.7 20.2 %collective-permute-start = (bf16[256,320]{1,0:T(8,128)(2,1)S(1)}, bf16[256,320]{1,0:T(8,128)(2,1)S(1)}, u32[]{:S(2)}, u32[]{:S(2)}) collective-permute-start(bf16[256,320]{1,0:T(8,128)(2,1)S(1)} %get-tuple-element.8), channel_id=1, source_target_pairs={{0,1},{1,0},{2,3},{3,2},{4,5},{5,4},{6,7},{7,6},{8,9},{9,8},{10,11... | collective-permute-start | bytes 491528 | tf_op jit(solution)/shard_map/ppermute | solution.py:320
  2.2 19.8 %collective-permute-start.1 = (bf16[256,320]{1,0:T(8,128)(2,1)S(1)}, bf16[256,320]{1,0:T(8,128)(2,1)S(1)}, u32[]{:S(2)}, u32[]{:S(2)}) collective-permute-start(bf16[256,320]{1,0:T(8,128)(2,1)S(1)} %get-tuple-element.9), channel_id=1, source_target_pairs={{1,2},{2,1},{3,4},{4,3},{5,6},{6,5},{7,8},{8,7},{9,10},{10,9},{11,... | collective-permute-start | bytes 491528 | tf_op jit(solution)/shard_map/ppermute | solution.py:321
  2.9 4.8 %collective-permute-start.2 = (f32[40,128]{1,0:T(8,128)S(1)}, f32[40,128]{1,0:T(8,128)S(1)}, u32[]{:S(2)}, u32[]{:S(2)}) collective-permute-start(f32[40,128]{1,0:T(8,128)S(1)} %get-tuple-element.10), channel_id=1, source_target_pairs={{0,1},{1,0},{2,3},{3,2},{4,5},{5,4},{6,7},{7,6},{8,9},{9,8},{10,11... | collective-permute-start | bytes 61448 | tf_op jit(solution)/shard_map/ppermute | solution.py:324
  7.7 3.8 %collective-permute-start.3 = (f32[40,128]{1,0:T(8,128)S(1)}, f32[40,128]{1,0:T(8,128)S(1)}, u32[]{:S(2)}, u32[]{:S(2)}) collective-permute-start(f32[40,128]{1,0:T(8,128)S(1)} %add.12), channel_id=1, source_target_pairs={{0,2},{1,3},{2,0},{3,1},{4,6},{5,7},{6,4},{7,5},{8,10},{9,11},{10,... | collective-permute-start | bytes 61448 | tf_op jit(solution)/shard_map/ppermute | solution.py:324
  11.5 5.3 %collective-permute-start.4 = (f32[40,128]{1,0:T(8,128)S(1)}, f32[40,128]{1,0:T(8,128)S(1)}, u32[]{:S(2)}, u32[]{:S(2)}) collective-permute-start(f32[40,128]{1,0:T(8,128)S(1)} %add.13), channel_id=1, source_target_pairs={{0,4},{1,5},{2,6},{3,7},{4,0},{5,1},{6,2},{7,3},{8,12},{9,13},{10,... | collective-permute-start | bytes 61448 | tf_op jit(solution)/shard_map/ppermute | solution.py:324
  16.7 5.2 %collective-permute-start.5 = (f32[40,128]{1,0:T(8,128)S(1)}, f32[40,128]{1,0:T(8,128)S(1)}, u32[]{:S(2)}, u32[]{:S(2)}) collective-permute-start(f32[40,128]{1,0:T(8,128)S(1)} %add.14), channel_id=1, source_target_pairs={{0,8},{1,9},{2,10},{3,11},{4,12},{5,13},{6,14},{7,15},{8,0},{9,1},... | collective-permute-start | bytes 61448 | tf_op jit(solution)/shard_map/ppermute | solution.py:324
  22.0 1.6 %copy-start = (bf16[3,3,320,320]{3,2,1,0:T(8,128)(2,1)S(1)}, bf16[3,3,320,320]{3,2,1,0:T(8,128)(2,1)}, u32[]{:S(2)}) copy-start(bf16[3,3,320,320]{3,2,1,0:T(8,128)(2,1)} %w_hbm.1) | copy-start | bytes 5529604
  23.6 1.0 %copy-start.2 = (bf16[32,16,320]{2,1,0:T(8,128)(2,1)S(1)}, bf16[32,16,320]{2,1,0:T(8,128)(2,1)}, u32[]{:S(2)}) copy-start(bf16[32,16,320]{2,1,0:T(8,128)(2,1)} %param.5) | copy-start | bytes 983044

commit v2 on v1

--- a/solution.py
+++ b/solution.py
@@ -39,7 +39,7 @@
     stride_blocks = STRIDE // cols
     tile_blocks = TILE // cols
 
-    def kernel(x_ref, stats_ref, ea_ref, eb_ref, s_ref, q_ref):
+    def kernel(x_ref, stats_ref, ea_ref, eb_ref, near_ref, s_ref, q_ref):
         block = lax.axis_index("wide")
         even = lax.rem(block, 2) == 0
         for a in range(0, DIL, 2):
@@ -49,7 +49,9 @@
                 pa, pb = [], []
                 for u in range(2):
                     r = rr * DIL + a + u
-                    x = x_ref[r * cols : (r + 1) * cols, :].astype(F32)
+                    x = x_ref[r * cols : (r + 1) * cols, :]
+                    near_ref[r * cols : (r + 1) * cols, :] = x
+                    x = x.astype(F32)
                     lo, hi = x[:8], x[8:]
                     s[u] += lo + hi
                     q[u] += lo * lo + hi * hi
@@ -90,6 +92,7 @@
             jax.ShapeDtypeStruct((32 + tile_rows, 128), F32),
             jax.ShapeDtypeStruct((rows * 8, channels), BF16),
             jax.ShapeDtypeStruct((rows * 8, channels), BF16),
+            jax.ShapeDtypeStruct((rows * cols, channels), BF16),
         ),
         scratch_shapes=[
             pltpu.VMEM((64, channels), F32),
@@ -114,8 +117,8 @@
     all_rows = 32 + tile_rows
 
     def kernel(
-        x_ref, ha_ref, hb_ref, stats_ref, gain_ref, shift_ref, bias_ref, w_hbm, o_ref,
-        w_ref, a_ref, sub_ref, blend_ref, sc_ref, sh_ref, tsc_ref, tsh_ref, bw_ref, sem,
+        x_ref, ha_ref, hb_ref, stats_ref, vec_ref, w_hbm, o_ref,
+        w_ref, bw_ref, sem, a_ref, sub_ref, blend_ref, sc_ref, sh_ref, tsc_ref, tsh_ref,
     ):
         copies = []
         for tap in range(9):
@@ -157,8 +160,8 @@
         mean = jnp.where(valid, mean, 0.0)
         inverse = jnp.where(valid, inverse, 0.0)
         both = jnp.concatenate([mean, inverse], axis=0)
-        gain = 0.5 * gain_ref[...]
-        shift = 0.5 * shift_ref[...]
+        gain = vec_ref[0:1, :]
+        shift = vec_ref[1:2, :]
         for half in range(2):
             wide = jnp.dot(
                 both,
@@ -179,6 +182,16 @@
                             jnp.where(pick, values[32:], 0.0), axis=0, keepdims=True
                         )
                         ref[8 * t : 8 * t + 8, :] = jnp.broadcast_to(line, (8, channels))
+
+        left_ok = jnp.where(block > 0, 1.0, 0.0).astype(F32)
+        right_ok = jnp.where(block < count - 1, 1.0, 0.0).astype(F32)
+
+        for r in range(DIL):
+            sub_ref[r] = jnp.zeros((4 * 8, channels), F32)
+            sub_ref[rows + DIL + r] = jnp.zeros((4 * 8, channels), F32)
+        for j in range(3):
+            blend_ref[j, 0] = jnp.zeros((cols, channels), F32)
+            blend_ref[j, rows + 1] = jnp.zeros((cols, channels), F32)
 
         sub_id = iota((8, channels), 0)
         for k in range(3):
@@ -201,16 +214,6 @@
                     q = col - (tid * STRIDE - rim)
                     ok = (q >= 0) & (q < TILE) & in_image
                     bw_ref[j, k, t] = jnp.where(ok, ramps[t] / whole, 0.0)
-
-        left_ok = jnp.where(block > 0, 1.0, 0.0).astype(F32)
-        right_ok = jnp.where(block < count - 1, 1.0, 0.0).astype(F32)
-
-        for r in range(DIL):
-            sub_ref[r] = jnp.zeros((4 * 8, channels), F32)
-            sub_ref[rows + DIL + r] = jnp.zeros((4 * 8, channels), F32)
-        for j in range(3):
-            blend_ref[j, 0] = jnp.zeros((cols, channels), F32)
-            blend_ref[j, rows + 1] = jnp.zeros((cols, channels), F32)
 
         def silu(x, scale, offset):
             h = x * scale + offset
@@ -275,20 +278,22 @@
                         a_ref[at, base : base + rem] = v[:, main:]
             return carry
 
-        lax.fori_loop(0, rows, gather, 0)
+        lax.fori_loop(0, rows, gather, 0, unroll=8)
         for c in copies:
             c.wait()
         acc = jnp.dot(a_ref[...], w_ref[...], preferred_element_type=F32)
-        o_ref[...] = (0.5 * acc + bias_ref[...]).astype(BF16)
+        o_ref[...] = (0.5 * acc + vec_ref[2:3, :]).astype(BF16)
 
     vmem = pl.BlockSpec(memory_space=pltpu.VMEM)
     return pl.pallas_call(
         kernel,
-        in_specs=[vmem] * 7 + [pl.BlockSpec(memory_space=pl.ANY)],
+        in_specs=[vmem] * 5 + [pl.BlockSpec(memory_space=pltpu.HBM)],
         out_specs=vmem,
         out_shape=jax.ShapeDtypeStruct((pixels, out_channels), BF16),
         scratch_shapes=[
             pltpu.VMEM((depth, out_channels), BF16),
+            pltpu.VMEM((3, 3, 2, 8, channels), F32),
+            pltpu.SemaphoreType.DMA((18,)),
             pltpu.VMEM((pixels, depth), BF16),
             pltpu.VMEM((rows + 2 * DIL, 4 * 8, channels), F32),
             pltpu.VMEM((3, rows + 2, cols, channels), F32),
@@ -296,10 +301,8 @@
             pltpu.VMEM((64, channels), F32),
             pltpu.VMEM((16, channels), F32),
             pltpu.VMEM((16, channels), F32),
-            pltpu.VMEM((3, 3, 2, 8, channels), F32),
-            pltpu.SemaphoreType.DMA((18,)),
         ],
-        compiler_params=pltpu.CompilerParams(vmem_limit_bytes=40 * 2**20),
+        compiler_params=pltpu.CompilerParams(vmem_limit_bytes=52 * 2**20),
         name="norm_conv",
     )
 
@@ -312,19 +315,26 @@
         tiles = -(-(count + (OVER // 2) // cols) // stride_blocks)
         tile_rows = -(-tiles // 8) * 8
         x = latent.reshape(rows * cols, channels)
-        stats, edge_a, edge_b = make_stats(rows, cols, channels, tile_rows)(x)
+        stats, edge_a, edge_b, x_near = make_stats(rows, cols, channels, tile_rows)(x)
         pairs_a = [(i, i ^ 1) for i in range(count)]
         pairs_b = []
         for i in range(1, count - 1, 2):
             pairs_b += [(i, i + 1), (i + 1, i)]
         halo_a = lax.ppermute(edge_a, "wide", pairs_a)
-        halo_b = lax.ppermute(edge_b, "wide", pairs_b)
+
+        def summed(stats, step):
+            return stats + lax.ppermute(stats, "wide", [(i, i ^ step) for i in range(count)])
+
+        vectors = jnp.stack([0.5 * gain, 0.5 * shift, bias])
         step = 1
         while step < count:
-            stats = stats + lax.ppermute(stats, "wide", [(i, i ^ step) for i in range(count)])
+            stats = summed(stats, step)
+            if step == 2:
+                edge_b, stats = lax.optimization_barrier((edge_b, stats))
+                halo_b = lax.ppermute(edge_b, "wide", pairs_b)
             step *= 2
         out = make_main(rows, cols, channels, out_channels, tile_rows, count)(
-            x, halo_a, halo_b, stats, gain[None], shift[None], bias[None], weight
+            x_near, halo_a, halo_b, stats, vectors, weight
         )
         return out.reshape(rows, cols, out_channels)
 

time: 34.7 us -> 23.7 us (0.68)
  Pallas kernels: 10.6 us -> 6.04 us
  local copies, waits for them, and re-layouts: 5.66 us -> 1.68 us
  starting transfers between devices: 13.3 us -> 10 us
  other arithmetic: 0.02 us -> 1.4 us
  waiting for transfers between devices: 4.87 us -> 4.26 us
    pallas_call x1, Pallas kernels: 9.82 us -> 5.28 us  [local(): make_main(rows, cols, channels, out_channels, tile_rows, count)]
    ppermute x4, starting transfers between devices: 12.2 us -> 9.3 us  [summed(): lax.ppermute(stats, 'wide', [(i, i ^ step) for i in range(count)])]
    unnamed x6 -> x2, local copies, waits for them, and re-layouts: 3.61 us -> 1 us
    broadcast_in_dim x3 -> x0, local copies, waits for them, and re-layouts: 2.05 us -> none  [the longest x1 0.68 us: local(): shift[None]]
    mul x0 -> x2, other arithmetic: none -> 1.37 us  [local(): vectors = jnp.stack([0.5 * gain, 0.5 * shift, bias])]
    another operation x0 -> x3, local copies, waits for them, and re-layouts: none -> 0.69 us  [local(): vectors = jnp.stack([0.5 * gain, 0.5 * shift, bias])]
    ppermute x4, waiting for transfers between devices: 4.87 us -> 4.26 us  [summed(): lax.ppermute(stats, 'wide', [(i, i ^ step) for i in range(count)])]
    ppermute x1, starting transfers between devices: 0.46 us -> 0.08 us  [local(): halo_a = lax.ppermute(edge_a, 'wide', pairs_a)]
  transfers between devices with their start and end apart: 6 -> 6, of which waited for: 3 -> 3; matrix products, arithmetic and copies ran while one was open for 6% -> 9% of each run, Pallas kernels for 0% -> 0%
where the time goes in v2:
time: 23.7 us; the launch traced here: 23.5 us
  starting transfers between devices  10 us (42%)
  Pallas kernels  6.04 us (25%)
  waiting for transfers between devices  4.26 us (18%)
  local copies, waits for them, and re-layouts  1.68 us (7%)
  other arithmetic  1.4 us (6%)
    ppermute x4, starting transfers between devices, summed(): lax.ppermute(stats, 'wide', [(i, i ^ step) for i in range(count)])  9.3 us
    pallas_call x1, Pallas kernels, local(): make_main(rows, cols, channels, out_channels, tile_rows, count)  5.28 us
    ppermute x4, waiting for transfers between devices, summed(): lax.ppermute(stats, 'wide', [(i, i ^ step) for i in range(count)])  4.26 us
    mul x2, other arithmetic, local(): vectors = jnp.stack([0.5 * gain, 0.5 * shift, bias])  1.37 us
    unnamed x2, local copies, waits for them, and re-layouts  1 us
    pallas_call x1, Pallas kernels, local(): make_stats(rows, cols, channels, tile_rows)(x)  0.75 us
    another operation x3, local copies, waits for them, and re-layouts, local(): vectors = jnp.stack([0.5 * gain, 0.5 * shift, bias])  0.69 us
    ppermute x1, starting transfers between devices, local(): halo_b = lax.ppermute(edge_b, 'wide', pairs_b)  0.66 us
  transfers between devices with their start and end apart: 6, of which 3 were waited for; matrix products, arithmetic and copies ran while one was open for 9% of the time, Pallas kernels for 0%

profile of v2, /device:TPU:0, one launch (start us, length us, event | category | flops | bytes accessed | tf_op | source)
XLA Modules:
  0.0 23.5 jit_solution(2537387192224360278)
XLA Ops:
  0.0 0.0 copy-start
  0.0 1.0 %copy-done = bf16[32,16,320]{2,1,0:T(8,128)(2,1)S(1)} copy-done((bf16[32,16,320]{2,1,0:T(8,128)(2,1)S(1)}, bf16[32,16,320]{2,1,0:T(8,128)(2,1)}, u32[]{:S(2)}) %copy-start) | copy-done | bytes 327704
  1.0 0.8 %block_stats.1 = (f32[40,128]{1,0:T(8,128)S(1)}, bf16[256,320]{1,0:T(8,128)(2,1)S(1)}, bf16[256,320]{1,0:T(8,128)(2,1)S(1)}, bf16[512,320]{1,0:T(8,128)(2,1)S(1)}) custom-call(bf16[512,320]{1,0:T(8,128)(2,1)S(1)} %bitcast.2), custom_call_target="tpu_custom_call" | custom-call | tf_op jit(solution)/shard_map/block_stats/pallas_call | solution.py:318
  1.8 0.5 %collective-permute-start.1 = (f32[40,128]{1,0:T(8,128)S(1)}, f32[40,128]{1,0:T(8,128)S(1)}, u32[]{:S(2)}, u32[]{:S(2)}) collective-permute-start(f32[40,128]{1,0:T(8,128)S(1)} %get-tuple-element.14), channel_id=1, source_target_pairs={{0,1},{1,0},{2,3},{3,2},{4,5},{5,4},{6,7},{7,6},{8,9},{9,8},{10,11... | collective-permute-start | bytes 61448 | tf_op jit(solution)/shard_map/ppermute | solution.py:326
  2.2 0.1 collective-permute-start
  2.3 0.8 %collective-permute-done.1 = f32[40,128]{1,0:T(8,128)S(1)} collective-permute-done((f32[40,128]{1,0:T(8,128)S(1)}, f32[40,128]{1,0:T(8,128)S(1)}, u32[]{:S(2)}, u32[]{:S(2)}) %collective-permute-start.1) | collective-permute-done | bytes 20512 | tf_op jit(solution)/shard_map/ppermute | solution.py:326
  3.1 2.9 %collective-permute-start.2 = (f32[40,128]{1,0:T(8,128)S(1)}, f32[40,128]{1,0:T(8,128)S(1)}, u32[]{:S(2)}, u32[]{:S(2)}) collective-permute-start(f32[40,128]{1,0:T(8,128)S(1)} %add.12), channel_id=1, source_target_pairs={{0,2},{1,3},{2,0},{3,1},{4,6},{5,7},{6,4},{7,5},{8,10},{9,11},{10,... | collective-permute-start | bytes 61448 | tf_op jit(solution)/shard_map/ppermute | solution.py:326
  5.9 0.7 %broadcast_multiply_fusion.1 = f32[320]{0:T(512)S(1)} fusion(f32[320]{0:T(512)} %param.6), kind=kLoop, calls=%fused_computation.2 | loop fusion | flops 320 | bytes 2560 | tf_op jit(solution)/shard_map/mul | solution.py:328
  6.6 1.1 %collective-permute-done.2 = f32[40,128]{1,0:T(8,128)S(1)} collective-permute-done((f32[40,128]{1,0:T(8,128)S(1)}, f32[40,128]{1,0:T(8,128)S(1)}, u32[]{:S(2)}, u32[]{:S(2)}) %collective-permute-start.2) | collective-permute-done | bytes 20512 | tf_op jit(solution)/shard_map/ppermute | solution.py:326
  7.7 2.1 %collective-permute-start.4 = (f32[40,128]{1,0:T(8,128)S(1)}, f32[40,128]{1,0:T(8,128)S(1)}, u32[]{:S(2)}, u32[]{:S(2)}) collective-permute-start(f32[40,128]{1,0:T(8,128)S(1)} %add.13), channel_id=1, source_target_pairs={{0,4},{1,5},{2,6},{3,7},{4,0},{5,1},{6,2},{7,3},{8,12},{9,13},{10,... | collective-permute-start | bytes 61448 | tf_op jit(solution)/shard_map/ppermute | solution.py:326
  9.8 0.7 %collective-permute-start.3 = (bf16[256,320]{1,0:T(8,128)(2,1)S(1)}, bf16[256,320]{1,0:T(8,128)(2,1)S(1)}, u32[]{:S(2)}, u32[]{:S(2)}) collective-permute-start(bf16[256,320]{1,0:T(8,128)(2,1)S(1)} %get-tuple-element.15), channel_id=1, source_target_pairs={{1,2},{2,1},{3,4},{4,3},{5,6},{6,5},{7,8},{8,7},{9,10},{10,9},{11,... | collective-permute-start | bytes 491528 | tf_op jit(solution)/shard_map/ppermute | solution.py:334
  10.4 0.7 %broadcast_multiply_fusion = f32[320]{0:T(512)S(1)} fusion(f32[320]{0:T(512)} %param.7), kind=kLoop, calls=%fused_computation.1 | loop fusion | flops 320 | bytes 2560 | tf_op jit(solution)/shard_map/mul | solution.py:328
  11.1 0.7 %stack.14 = f32[1,320]{1,0:T(1,128)S(1)} reshape(f32[320]{0:T(512)} %param.9) | data formatting | bytes 2560 | tf_op jit(solution)/shard_map/stack | solution.py:328
  11.8 0.0 collective-permute-done.4
  11.8 3.9 %collective-permute-start.5 = (f32[40,128]{1,0:T(8,128)S(1)}, f32[40,128]{1,0:T(8,128)S(1)}, u32[]{:S(2)}, u32[]{:S(2)}) collective-permute-start(f32[40,128]{1,0:T(8,128)S(1)} %add.14), channel_id=1, source_target_pairs={{0,8},{1,9},{2,10},{3,11},{4,12},{5,13},{6,14},{7,15},{8,0},{9,1},... | collective-permute-start | bytes 61448 | tf_op jit(solution)/shard_map/ppermute | solution.py:326
  15.7 2.4 %collective-permute-done.5 = f32[40,128]{1,0:T(8,128)S(1)} collective-permute-done((f32[40,128]{1,0:T(8,128)S(1)}, f32[40,128]{1,0:T(8,128)S(1)}, u32[]{:S(2)}, u32[]{:S(2)}) %collective-permute-start.5) | collective-permute-done | bytes 20512 | tf_op jit(solution)/shard_map/ppermute | solution.py:326
  18.2 0.0 collective-permute-done.ha_ref
  18.2 0.0 collective-permute-done.3.hb_ref
  18.2 5.3 %norm_conv.1 = bf16[512,320]{1,0:T(8,128)(2,1)} custom-call(bf16[512,320]{1,0:T(8,128)(2,1)S(1)} %get-tuple-element.11.x_ref, bf16[256,320]{1,0:T(8,128)(2,1)S(1)} %collective-permute-done.ha_ref, bf16[256,320]{1,0:T(8,128)(2,1)S(1)} %collective-permute-done.3.hb_ref, f32[40,128]{1,0:T(8,128)S(1)} %add.15.stats_ref, f32[3,320]{1,0:T(4,128)S(1)} %pad_maximum_fusion.vec_ref, ...), custom_call_target="tpu_custom_call" | custom-call | tf_op jit(solution)/shard_map/norm_conv/pallas_call | solution.py:336
  (7 shorter events, 0.0 us)
Async XLA Ops:
  0.0 1.0 %copy-start = (bf16[32,16,320]{2,1,0:T(8,128)(2,1)S(1)}, bf16[32,16,320]{2,1,0:T(8,128)(2,1)}, u32[]{:S(2)}) copy-start(bf16[32,16,320]{2,1,0:T(8,128)(2,1)} %param.5) | copy-start | bytes 983044
  1.8 1.3 %collective-permute-start.1 = (f32[40,128]{1,0:T(8,128)S(1)}, f32[40,128]{1,0:T(8,128)S(1)}, u32[]{:S(2)}, u32[]{:S(2)}) collective-permute-start(f32[40,128]{1,0:T(8,128)S(1)} %get-tuple-element.14), channel_id=1, source_target_pairs={{0,1},{1,0},{2,3},{3,2},{4,5},{5,4},{6,7},{7,6},{8,9},{9,8},{10,11... | collective-permute-start | bytes 61448 | tf_op jit(solution)/shard_map/ppermute | solution.py:326
  2.2 16.0 %collective-permute-start = (bf16[256,320]{1,0:T(8,128)(2,1)S(1)}, bf16[256,320]{1,0:T(8,128)(2,1)S(1)}, u32[]{:S(2)}, u32[]{:S(2)}) collective-permute-start(bf16[256,320]{1,0:T(8,128)(2,1)S(1)} %get-tuple-element.12), channel_id=1, source_target_pairs={{0,1},{1,0},{2,3},{3,2},{4,5},{5,4},{6,7},{7,6},{8,9},{9,8},{10,11... | collective-permute-start | bytes 491528 | tf_op jit(solution)/shard_map/ppermute | solution.py:323
  3.1 4.6 %collective-permute-start.2 = (f32[40,128]{1,0:T(8,128)S(1)}, f32[40,128]{1,0:T(8,128)S(1)}, u32[]{:S(2)}, u32[]{:S(2)}) collective-permute-start(f32[40,128]{1,0:T(8,128)S(1)} %add.12), channel_id=1, source_target_pairs={{0,2},{1,3},{2,0},{3,1},{4,6},{5,7},{6,4},{7,5},{8,10},{9,11},{10,... | collective-permute-start | bytes 61448 | tf_op jit(solution)/shard_map/ppermute | solution.py:326
  7.7 4.1 %collective-permute-start.4 = (f32[40,128]{1,0:T(8,128)S(1)}, f32[40,128]{1,0:T(8,128)S(1)}, u32[]{:S(2)}, u32[]{:S(2)}) collective-permute-start(f32[40,128]{1,0:T(8,128)S(1)} %add.13), channel_id=1, source_target_pairs={{0,4},{1,5},{2,6},{3,7},{4,0},{5,1},{6,2},{7,3},{8,12},{9,13},{10,... | collective-permute-start | bytes 61448 | tf_op jit(solution)/shard_map/ppermute | solution.py:326
  9.8 8.4 %collective-permute-start.3 = (bf16[256,320]{1,0:T(8,128)(2,1)S(1)}, bf16[256,320]{1,0:T(8,128)(2,1)S(1)}, u32[]{:S(2)}, u32[]{:S(2)}) collective-permute-start(bf16[256,320]{1,0:T(8,128)(2,1)S(1)} %get-tuple-element.15), channel_id=1, source_target_pairs={{1,2},{2,1},{3,4},{4,3},{5,6},{6,5},{7,8},{8,7},{9,10},{10,9},{11,... | collective-permute-start | bytes 491528 | tf_op jit(solution)/shard_map/ppermute | solution.py:334
  11.8 6.3 %collective-permute-start.5 = (f32[40,128]{1,0:T(8,128)S(1)}, f32[40,128]{1,0:T(8,128)S(1)}, u32[]{:S(2)}, u32[]{:S(2)}) collective-permute-start(f32[40,128]{1,0:T(8,128)S(1)} %add.14), channel_id=1, source_target_pairs={{0,8},{1,9},{2,10},{3,11},{4,12},{5,13},{6,14},{7,15},{8,0},{9,1},... | collective-permute-start | bytes 61448 | tf_op jit(solution)/shard_map/ppermute | solution.py:326

commit v3 on v2

--- a/solution.py
+++ b/solution.py
@@ -103,96 +103,13 @@
     )
 
 
-def make_main(rows, cols, channels, out_channels, tile_rows, count):
-    per_group = channels // NORM_GROUPS
+def make_blend(cols, channels, count):
     rim = OVER // 2
-    rim_blocks = rim // cols
-    stride_blocks = STRIDE // cols
-    tile_blocks = TILE // cols
-    pixels = rows * cols
-    main = (channels // 128) * 128
-    rem = channels - main
-    depth = 9 * channels
-    sub_items = float((rows // DIL) * (cols // DIL) * count * per_group)
-    all_rows = 32 + tile_rows
-
-    def kernel(
-        x_ref, ha_ref, hb_ref, stats_ref, vec_ref, w_hbm, o_ref,
-        w_ref, bw_ref, sem, a_ref, sub_ref, blend_ref, sc_ref, sh_ref, tsc_ref, tsh_ref,
-    ):
-        copies = []
-        for tap in range(9):
-            i, j = tap // 3, tap % 3
-            copies.append(
-                pltpu.make_async_copy(
-                    w_hbm.at[i, j, pl.ds(0, main), :],
-                    w_ref.at[pl.ds(tap * main, main), :],
-                    sem.at[2 * tap],
-                )
-            )
-            copies.append(
-                pltpu.make_async_copy(
-                    w_hbm.at[i, j, pl.ds(main, rem), :],
-                    w_ref.at[pl.ds(9 * main + tap * rem, rem), :],
-                    sem.at[2 * tap + 1],
-                )
-            )
-        for c in copies:
-            c.start()
-
+
+    def kernel(after_ref, bw_ref):
         block = lax.axis_index("wide")
-        even = lax.rem(block, 2) == 0
-        tile0 = lax.div(block + rim_blocks, stride_blocks)
+        tile0 = lax.div(block + rim // cols, STRIDE // cols)
         tile1 = tile0 - 1
-
-        stats = stats_ref[...]
-        row_id = iota((all_rows, 128), 0)
-        lane_id = iota((all_rows, 128), 1)
-        start = (row_id - 32) * stride_blocks - rim_blocks
-        blocks = jnp.minimum(start + tile_blocks, count) - jnp.maximum(start, 0)
-        tile_items = jnp.maximum(blocks, 1).astype(F32) * float(pixels * per_group)
-        is_sub = row_id < 32
-        items = jnp.where(is_sub, sub_items, tile_items)
-        mean = stats / items
-        square = pltpu.roll(stats, 64, 1) / items
-        inverse = lax.rsqrt(square - mean * mean + EPS)
-        valid = lane_id < jnp.where(is_sub, 64, 32)
-        mean = jnp.where(valid, mean, 0.0)
-        inverse = jnp.where(valid, inverse, 0.0)
-        both = jnp.concatenate([mean, inverse], axis=0)
-        gain = vec_ref[0:1, :]
-        shift = vec_ref[1:2, :]
-        for half in range(2):
-            wide = jnp.dot(
-                both,
-                group_onehot(channels, per_group, 32 * half),
-                precision=lax.Precision.HIGHEST,
-                preferred_element_type=F32,
-            )
-            scale = wide[all_rows:] * gain
-            offset = shift - wide[:all_rows] * scale
-            sc_ref[32 * half : 32 * half + 32, :] = scale[:32]
-            sh_ref[32 * half : 32 * half + 32, :] = offset[:32]
-            if half == 0:
-                tile_row = iota((tile_rows, channels), 0)
-                for t, tid in enumerate((tile0, tile1)):
-                    pick = tile_row == jnp.maximum(tid, 0)
-                    for ref, values in ((tsc_ref, scale), (tsh_ref, offset)):
-                        line = jnp.sum(
-                            jnp.where(pick, values[32:], 0.0), axis=0, keepdims=True
-                        )
-                        ref[8 * t : 8 * t + 8, :] = jnp.broadcast_to(line, (8, channels))
-
-        left_ok = jnp.where(block > 0, 1.0, 0.0).astype(F32)
-        right_ok = jnp.where(block < count - 1, 1.0, 0.0).astype(F32)
-
-        for r in range(DIL):
-            sub_ref[r] = jnp.zeros((4 * 8, channels), F32)
-            sub_ref[rows + DIL + r] = jnp.zeros((4 * 8, channels), F32)
-        for j in range(3):
-            blend_ref[j, 0] = jnp.zeros((cols, channels), F32)
-            blend_ref[j, rows + 1] = jnp.zeros((cols, channels), F32)
-
         sub_id = iota((8, channels), 0)
         for k in range(3):
             if k < 2:
@@ -215,6 +132,112 @@
                     ok = (q >= 0) & (q < TILE) & in_image
                     bw_ref[j, k, t] = jnp.where(ok, ramps[t] / whole, 0.0)
 
+
+    return pl.pallas_call(
+        kernel,
+        in_specs=[pl.BlockSpec(memory_space=pl.ANY)],
+        out_specs=pl.BlockSpec(memory_space=pltpu.VMEM),
+        out_shape=jax.ShapeDtypeStruct((3, 3, 2, 8, channels), F32),
+        compiler_params=pltpu.CompilerParams(vmem_limit_bytes=16 * 2**20),
+        cost_estimate=pl.CostEstimate(flops=5000000000, bytes_accessed=0, transcendentals=0),
+        name="blend_weights",
+    )
+
+
+def make_main(rows, cols, channels, out_channels, tile_rows, count):
+    per_group = channels // NORM_GROUPS
+    rim = OVER // 2
+    rim_blocks = rim // cols
+    stride_blocks = STRIDE // cols
+    tile_blocks = TILE // cols
+    pixels = rows * cols
+    main = (channels // 128) * 128
+    rem = channels - main
+    depth = 9 * channels
+    sub_items = float((rows // DIL) * (cols // DIL) * count * per_group)
+    all_rows = 32 + tile_rows
+
+    def kernel(
+        x_ref, ha_ref, hb_ref, stats_ref, vec_ref, bw_ref, w_hbm, o_ref,
+        w_ref, sem, a_ref, sub_ref, blend_ref, sc_ref, sh_ref, tsc_ref, tsh_ref,
+    ):
+        copies = []
+        for tap in range(9):
+            i, j = tap // 3, tap % 3
+            copies.append(
+                pltpu.make_async_copy(
+                    w_hbm.at[i, j, pl.ds(0, main), :],
+                    w_ref.at[pl.ds(tap * main, main), :],
+                    sem.at[2 * tap],
+                )
+            )
+            copies.append(
+                pltpu.make_async_copy(
+                    w_hbm.at[i, j, pl.ds(main, rem), :],
+                    w_ref.at[pl.ds(9 * main + tap * rem, rem), :],
+                    sem.at[2 * tap + 1],
+                )
+            )
+        for c in copies:
+            c.start()
+
+        block = lax.axis_index("wide")
+        even = lax.rem(block, 2) == 0
+        tile0 = lax.div(block + rim_blocks, stride_blocks)
+        tile1 = tile0 - 1
+
+        stats = stats_ref[...]
+        row_id = iota((all_rows, 128), 0)
+        lane_id = iota((all_rows, 128), 1)
+        start = (row_id - 32) * stride_blocks - rim_blocks
+        blocks = jnp.minimum(start + tile_blocks, count) - jnp.maximum(start, 0)
+        tile_items = jnp.maximum(blocks, 1).astype(F32) * float(pixels * per_group)
+        is_sub = row_id < 32
+        items = jnp.where(is_sub, sub_items, tile_items)
+        mean = stats / items
+        square = pltpu.roll(stats, 64, 1) / items
+        inverse = lax.rsqrt(square - mean * mean + EPS)
+        valid = lane_id < jnp.where(is_sub, 64, 32)
+        mean = jnp.where(valid, mean, 0.0)
+        inverse = jnp.where(valid, inverse, 0.0)
+        both = jnp.concatenate([mean, inverse], axis=0)
+        vec = vec_ref[...].reshape(1, -1)
+        wide_c = vec.shape[1] // 3
+        gain = 0.5 * vec[:, :channels]
+        shift = 0.5 * vec[:, wide_c : wide_c + channels]
+        bias = vec[:, 2 * wide_c : 2 * wide_c + channels]
+        for half in range(2):
+            wide = jnp.dot(
+                both,
+                group_onehot(channels, per_group, 32 * half),
+                precision=lax.Precision.HIGHEST,
+                preferred_element_type=F32,
+            )
+            scale = wide[all_rows:] * gain
+            offset = shift - wide[:all_rows] * scale
+            sc_ref[32 * half : 32 * half + 32, :] = scale[:32]
+            sh_ref[32 * half : 32 * half + 32, :] = offset[:32]
+            if half == 0:
+                tile_row = iota((tile_rows, channels), 0)
+                for t, tid in enumerate((tile0, tile1)):
+                    pick = tile_row == jnp.maximum(tid, 0)
+                    for ref, values in ((tsc_ref, scale), (tsh_ref, offset)):
+                        line = jnp.sum(
+                            jnp.where(pick, values[32:], 0.0), axis=0, keepdims=True
+                        )
+                        ref[8 * t : 8 * t + 8, :] = jnp.broadcast_to(line, (8, channels))
+
+        left_ok = jnp.where(block > 0, 1.0, 0.0).astype(F32)
+        right_ok = jnp.where(block < count - 1, 1.0, 0.0).astype(F32)
+
+        for r in range(DIL):
+            sub_ref[r] = jnp.zeros((4 * 8, channels), F32)
+            sub_ref[rows + DIL + r] = jnp.zeros((4 * 8, channels), F32)
+        for j in range(3):
+            blend_ref[j, 0] = jnp.zeros((cols, channels), F32)
+            blend_ref[j, rows + 1] = jnp.zeros((cols, channels), F32)
+
+        sub_id = iota((8, channels), 0)
         def silu(x, scale, offset):
             h = x * scale + offset
             return h + h * jnp.tanh(h)
@@ -278,21 +301,23 @@
                         a_ref[at, base : base + rem] = v[:, main:]
             return carry
 
-        lax.fori_loop(0, rows, gather, 0, unroll=8)
         for c in copies:
             c.wait()
-        acc = jnp.dot(a_ref[...], w_ref[...], preferred_element_type=F32)
-        o_ref[...] = (0.5 * acc + vec_ref[2:3, :]).astype(BF16)
+        for m in range(0, rows, 8):
+            for r in range(m, m + 8):
+                gather(r, 0)
+            at = pl.ds(m * cols, 8 * cols)
+            acc = jnp.dot(a_ref[at, :], w_ref[...], preferred_element_type=F32)
+            o_ref[at, :] = (0.5 * acc + bias).astype(BF16)
 
     vmem = pl.BlockSpec(memory_space=pltpu.VMEM)
     return pl.pallas_call(
         kernel,
-        in_specs=[vmem] * 5 + [pl.BlockSpec(memory_space=pltpu.HBM)],
+        in_specs=[vmem] * 6 + [pl.BlockSpec(memory_space=pltpu.HBM)],
         out_specs=vmem,
         out_shape=jax.ShapeDtypeStruct((pixels, out_channels), BF16),
         scratch_shapes=[
             pltpu.VMEM((depth, out_channels), BF16),
-            pltpu.VMEM((3, 3, 2, 8, channels), F32),
             pltpu.SemaphoreType.DMA((18,)),
             pltpu.VMEM((pixels, depth), BF16),
             pltpu.VMEM((rows + 2 * DIL, 4 * 8, channels), F32),
@@ -325,16 +350,20 @@
         def summed(stats, step):
             return stats + lax.ppermute(stats, "wide", [(i, i ^ step) for i in range(count)])
 
-        vectors = jnp.stack([0.5 * gain, 0.5 * shift, bias])
+        spare = jnp.zeros((-channels % 128,), F32)
+        vectors = jnp.concatenate([gain, spare, shift, spare, bias, spare])
         step = 1
         while step < count:
             stats = summed(stats, step)
             if step == 2:
+                blend, stats = lax.optimization_barrier((blend, stats))
+            if step == 1:
                 edge_b, stats = lax.optimization_barrier((edge_b, stats))
                 halo_b = lax.ppermute(edge_b, "wide", pairs_b)
+                blend = make_blend(cols, channels, count)(stats)
             step *= 2
         out = make_main(rows, cols, channels, out_channels, tile_rows, count)(
-            x_near, halo_a, halo_b, stats, vectors, weight
+            x_near, halo_a, halo_b, stats, vectors, blend, weight
         )
         return out.reshape(rows, cols, out_channels)
 

time: 23.7 us -> 23 us (0.970)
  waiting for transfers between devices: 4.26 us -> 7.5 us
  other arithmetic: 1.4 us -> 0.02 us
  starting transfers between devices: 10 us -> 8.79 us
  Pallas kernels: 6.04 us -> 5.38 us
  local copies, waits for them, and re-layouts: 1.68 us -> 1.09 us
    ppermute x4, waiting for transfers between devices: 4.26 us -> 7.5 us  [summed(): lax.ppermute(stats, 'wide', [(i, i ^ step) for i in range(count)])]
    mul x2 -> x0, other arithmetic: 1.37 us -> none  [local(): vectors = jnp.stack([0.5 * gain, 0.5 * shift, bias])]
    ppermute x4, starting transfers between devices: 9.3 us -> 8.05 us  [summed(): lax.ppermute(stats, 'wide', [(i, i ^ step) for i in range(count)])]
    pallas_call x1, Pallas kernels: 5.28 us -> 4.56 us  [local(): make_main(rows, cols, channels, out_channels, tile_rows, count)]
    another operation x3 -> x0, local copies, waits for them, and re-layouts: 0.69 us -> none  [local(): vectors = jnp.stack([0.5 * gain, 0.5 * shift, bias])]
    unnamed x2 -> x8, local copies, waits for them, and re-layouts: 1 us -> 1.01 us
  transfers between devices with their start and end apart: 6 -> 6, of which waited for: 3 -> 4; matrix products, arithmetic and copies ran while one was open for 9% -> 0% of each run, Pallas kernels for 0% -> 0%
where the time goes in v3:
time: 23 us; the launch traced here: 22.8 us
  starting transfers between devices  8.79 us (38%)
  waiting for transfers between devices  7.5 us (33%)
  Pallas kernels  5.38 us (23%)
  local copies, waits for them, and re-layouts  1.09 us (5%)
    ppermute x4, starting transfers between devices, summed(): lax.ppermute(stats, 'wide', [(i, i ^ step) for i in range(count)])  8.05 us
    ppermute x4, waiting for transfers between devices, summed(): lax.ppermute(stats, 'wide', [(i, i ^ step) for i in range(count)])  7.5 us
    pallas_call x1, Pallas kernels, local(): make_main(rows, cols, channels, out_channels, tile_rows, count)  4.56 us
    unnamed x8, local copies, waits for them, and re-layouts  1.01 us
    pallas_call x1, Pallas kernels, local(): make_stats(rows, cols, channels, tile_rows)(x)  0.75 us
    ppermute x1, starting transfers between devices, local(): halo_b = lax.ppermute(edge_b, 'wide', pairs_b)  0.66 us
  transfers between devices with their start and end apart: 6, of which 4 were waited for; matrix products, arithmetic and copies ran while one was open for 0% of the time, Pallas kernels for 0%

profile of v3, /device:TPU:0, one launch (start us, length us, event | category | flops | bytes accessed | tf_op | source)
XLA Modules:
  0.0 22.8 jit_solution(16999525504230667512)
XLA Ops:
  0.0 0.0 copy-start
  0.0 1.0 %copy-done = bf16[32,16,320]{2,1,0:T(8,128)(2,1)S(1)} copy-done((bf16[32,16,320]{2,1,0:T(8,128)(2,1)S(1)}, bf16[32,16,320]{2,1,0:T(8,128)(2,1)}, u32[]{:S(2)}) %copy-start) | copy-done | bytes 327704
  1.0 0.8 %block_stats.1 = (f32[40,128]{1,0:T(8,128)S(1)}, bf16[256,320]{1,0:T(8,128)(2,1)S(1)}, bf16[256,320]{1,0:T(8,128)(2,1)S(1)}, bf16[512,320]{1,0:T(8,128)(2,1)S(1)}) custom-call(bf16[512,320]{1,0:T(8,128)(2,1)S(1)} %bitcast.2), custom_call_target="tpu_custom_call" | custom-call | tf_op jit(solution)/shard_map/block_stats/pallas_call | solution.py:343
  1.8 0.5 %collective-permute-start.1 = (f32[40,128]{1,0:T(8,128)S(1)}, f32[40,128]{1,0:T(8,128)S(1)}, u32[]{:S(2)}, u32[]{:S(2)}) collective-permute-start(f32[40,128]{1,0:T(8,128)S(1)} %get-tuple-element.16), channel_id=1, source_target_pairs={{0,1},{1,0},{2,3},{3,2},{4,5},{5,4},{6,7},{7,6},{8,9},{9,8},{10,11... | collective-permute-start | bytes 61448 | tf_op jit(solution)/shard_map/ppermute | solution.py:351
  2.2 0.1 collective-permute-start
  2.3 0.8 %collective-permute-done.1 = f32[40,128]{1,0:T(8,128)S(1)} collective-permute-done((f32[40,128]{1,0:T(8,128)S(1)}, f32[40,128]{1,0:T(8,128)S(1)}, u32[]{:S(2)}, u32[]{:S(2)}) %collective-permute-start.1) | collective-permute-done | bytes 20512 | tf_op jit(solution)/shard_map/ppermute | solution.py:351
  3.1 0.0 copy-start.1
  3.1 0.0 copy-start.2
  3.1 0.0 copy-start.3
  3.1 2.9 %collective-permute-start.3 = (f32[40,128]{1,0:T(8,128)S(1)}, f32[40,128]{1,0:T(8,128)S(1)}, u32[]{:S(2)}, u32[]{:S(2)}) collective-permute-start(f32[40,128]{1,0:T(8,128)S(1)} %add.12.after_ref), channel_id=1, source_target_pairs={{0,2},{1,3},{2,0},{3,1},{4,6},{5,7},{6,4},{7,5},{8,10},{9,11},{10,... | collective-permute-start | bytes 61448 | tf_op jit(solution)/shard_map/ppermute | solution.py:351
  6.0 0.7 %collective-permute-start.2 = (bf16[256,320]{1,0:T(8,128)(2,1)S(1)}, bf16[256,320]{1,0:T(8,128)(2,1)S(1)}, u32[]{:S(2)}, u32[]{:S(2)}) collective-permute-start(bf16[256,320]{1,0:T(8,128)(2,1)S(1)} %get-tuple-element.17), channel_id=1, source_target_pairs={{1,2},{2,1},{3,4},{4,3},{5,6},{6,5},{7,8},{8,7},{9,10},{10,9},{11,... | collective-permute-start | bytes 491528 | tf_op jit(solution)/shard_map/ppermute | solution.py:362
  6.7 0.1 blend_weights.1.bw_ref
  6.7 1.0 %collective-permute-done.3 = f32[40,128]{1,0:T(8,128)S(1)} collective-permute-done((f32[40,128]{1,0:T(8,128)S(1)}, f32[40,128]{1,0:T(8,128)S(1)}, u32[]{:S(2)}, u32[]{:S(2)}) %collective-permute-start.3) | collective-permute-done | bytes 20512 | tf_op jit(solution)/shard_map/ppermute | solution.py:351
  7.8 2.1 %collective-permute-start.4 = (f32[40,128]{1,0:T(8,128)S(1)}, f32[40,128]{1,0:T(8,128)S(1)}, u32[]{:S(2)}, u32[]{:S(2)}) collective-permute-start(f32[40,128]{1,0:T(8,128)S(1)} %add.13), channel_id=1, source_target_pairs={{0,4},{1,5},{2,6},{3,7},{4,0},{5,1},{6,2},{7,3},{8,12},{9,13},{10,... | collective-permute-start | bytes 61448 | tf_op jit(solution)/shard_map/ppermute | solution.py:351
  9.8 3.7 %collective-permute-done.4 = f32[40,128]{1,0:T(8,128)S(1)} collective-permute-done((f32[40,128]{1,0:T(8,128)S(1)}, f32[40,128]{1,0:T(8,128)S(1)}, u32[]{:S(2)}, u32[]{:S(2)}) %collective-permute-start.4) | collective-permute-done | bytes 20512 | tf_op jit(solution)/shard_map/ppermute | solution.py:351
  13.6 2.6 %collective-permute-start.5 = (f32[40,128]{1,0:T(8,128)S(1)}, f32[40,128]{1,0:T(8,128)S(1)}, u32[]{:S(2)}, u32[]{:S(2)}) collective-permute-start(f32[40,128]{1,0:T(8,128)S(1)} %add.14), channel_id=1, source_target_pairs={{0,8},{1,9},{2,10},{3,11},{4,12},{5,13},{6,14},{7,15},{8,0},{9,1},... | collective-permute-start | bytes 61448 | tf_op jit(solution)/shard_map/ppermute | solution.py:351
  16.2 0.0 copy-done.1
  16.2 0.0 copy-done.2
  16.2 0.0 copy-done.3
  16.2 0.1 concatenate.3.vec_ref
  16.2 2.0 %collective-permute-done.5 = f32[40,128]{1,0:T(8,128)S(1)} collective-permute-done((f32[40,128]{1,0:T(8,128)S(1)}, f32[40,128]{1,0:T(8,128)S(1)}, u32[]{:S(2)}, u32[]{:S(2)}) %collective-permute-start.5) | collective-permute-done | bytes 20512 | tf_op jit(solution)/shard_map/ppermute | solution.py:351
  18.2 0.0 collective-permute-done.ha_ref
  18.3 0.0 collective-permute-done.2.hb_ref
  18.3 4.6 %norm_conv.1 = bf16[512,320]{1,0:T(8,128)(2,1)} custom-call(bf16[512,320]{1,0:T(8,128)(2,1)S(1)} %get-tuple-element.13.x_ref, bf16[256,320]{1,0:T(8,128)(2,1)S(1)} %collective-permute-done.ha_ref, bf16[256,320]{1,0:T(8,128)(2,1)S(1)} %collective-permute-done.2.hb_ref, f32[40,128]{1,0:T(8,128)S(1)} %add.15.stats_ref, f32[1152]{0:T(1024)S(1)} %concatenate.3.vec_ref, ...), custom_call_target="tpu_custom_call" | custom-call | tf_op jit(solution)/shard_map/norm_conv/pallas_call | solution.py:365
  (5 shorter events, 0.0 us)
Async XLA Ops:
  0.0 1.0 %copy-start = (bf16[32,16,320]{2,1,0:T(8,128)(2,1)S(1)}, bf16[32,16,320]{2,1,0:T(8,128)(2,1)}, u32[]{:S(2)}) copy-start(bf16[32,16,320]{2,1,0:T(8,128)(2,1)} %param.5) | copy-start | bytes 983044
  1.8 1.3 %collective-permute-start.1 = (f32[40,128]{1,0:T(8,128)S(1)}, f32[40,128]{1,0:T(8,128)S(1)}, u32[]{:S(2)}, u32[]{:S(2)}) collective-permute-start(f32[40,128]{1,0:T(8,128)S(1)} %get-tuple-element.16), channel_id=1, source_target_pairs={{0,1},{1,0},{2,3},{3,2},{4,5},{5,4},{6,7},{7,6},{8,9},{9,8},{10,11... | collective-permute-start | bytes 61448 | tf_op jit(solution)/shard_map/ppermute | solution.py:351
  2.2 16.0 %collective-permute-start = (bf16[256,320]{1,0:T(8,128)(2,1)S(1)}, bf16[256,320]{1,0:T(8,128)(2,1)S(1)}, u32[]{:S(2)}, u32[]{:S(2)}) collective-permute-start(bf16[256,320]{1,0:T(8,128)(2,1)S(1)} %get-tuple-element.14), channel_id=1, source_target_pairs={{0,1},{1,0},{2,3},{3,2},{4,5},{5,4},{6,7},{7,6},{8,9},{9,8},{10,11... | collective-permute-start | bytes 491528 | tf_op jit(solution)/shard_map/ppermute | solution.py:348
  3.1 13.1 %copy-start.1 = (f32[320]{0:T(512)S(1)}, f32[320]{0:T(512)}, u32[]{:S(2)}) copy-start(f32[320]{0:T(512)} %param.6) | copy-start | bytes 3844
  3.1 13.1 %copy-start.2 = (f32[320]{0:T(512)S(1)}, f32[320]{0:T(512)}, u32[]{:S(2)}) copy-start(f32[320]{0:T(512)} %param.7) | copy-start | bytes 3844
  3.1 13.1 %copy-start.3 = (f32[320]{0:T(512)S(1)}, f32[320]{0:T(512)}, u32[]{:S(2)}) copy-start(f32[320]{0:T(512)} %param.9) | copy-start | bytes 3844
  3.1 4.7 %collective-permute-start.3 = (f32[40,128]{1,0:T(8,128)S(1)}, f32[40,128]{1,0:T(8,128)S(1)}, u32[]{:S(2)}, u32[]{:S(2)}) collective-permute-start(f32[40,128]{1,0:T(8,128)S(1)} %add.12.after_ref), channel_id=1, source_target_pairs={{0,2},{1,3},{2,0},{3,1},{4,6},{5,7},{6,4},{7,5},{8,10},{9,11},{10,... | collective-permute-start | bytes 61448 | tf_op jit(solution)/shard_map/ppermute | solution.py:351
  6.0 12.3 %collective-permute-start.2 = (bf16[256,320]{1,0:T(8,128)(2,1)S(1)}, bf16[256,320]{1,0:T(8,128)(2,1)S(1)}, u32[]{:S(2)}, u32[]{:S(2)}) collective-permute-start(bf16[256,320]{1,0:T(8,128)(2,1)S(1)} %get-tuple-element.17), channel_id=1, source_target_pairs={{1,2},{2,1},{3,4},{4,3},{5,6},{6,5},{7,8},{8,7},{9,10},{10,9},{11,... | collective-permute-start | bytes 491528 | tf_op jit(solution)/shard_map/ppermute | solution.py:362
  7.8 5.8 %collective-permute-start.4 = (f32[40,128]{1,0:T(8,128)S(1)}, f32[40,128]{1,0:T(8,128)S(1)}, u32[]{:S(2)}, u32[]{:S(2)}) collective-permute-start(f32[40,128]{1,0:T(8,128)S(1)} %add.13), channel_id=1, source_target_pairs={{0,4},{1,5},{2,6},{3,7},{4,0},{5,1},{6,2},{7,3},{8,12},{9,13},{10,... | collective-permute-start | bytes 61448 | tf_op jit(solution)/shard_map/ppermute | solution.py:351
  13.6 4.7 %collective-permute-start.5 = (f32[40,128]{1,0:T(8,128)S(1)}, f32[40,128]{1,0:T(8,128)S(1)}, u32[]{:S(2)}, u32[]{:S(2)}) collective-permute-start(f32[40,128]{1,0:T(8,128)S(1)} %add.14), channel_id=1, source_target_pairs={{0,8},{1,9},{2,10},{3,11},{4,12},{5,13},{6,14},{7,15},{8,0},{9,1},... | collective-permute-start | bytes 61448 | tf_op jit(solution)/shard_map/ppermute | solution.py:351

commit v4 on v3

--- a/solution.py
+++ b/solution.py
@@ -144,23 +144,11 @@
     )
 
 
-def make_main(rows, cols, channels, out_channels, tile_rows, count):
-    per_group = channels // NORM_GROUPS
-    rim = OVER // 2
-    rim_blocks = rim // cols
-    stride_blocks = STRIDE // cols
-    tile_blocks = TILE // cols
-    pixels = rows * cols
+def make_weights(channels, out_channels):
     main = (channels // 128) * 128
     rem = channels - main
-    depth = 9 * channels
-    sub_items = float((rows // DIL) * (cols // DIL) * count * per_group)
-    all_rows = 32 + tile_rows
-
-    def kernel(
-        x_ref, ha_ref, hb_ref, stats_ref, vec_ref, bw_ref, w_hbm, o_ref,
-        w_ref, sem, a_ref, sub_ref, blend_ref, sc_ref, sh_ref, tsc_ref, tsh_ref,
-    ):
+
+    def kernel(after_ref, w_hbm, w_ref, sem):
         copies = []
         for tap in range(9):
             i, j = tap // 3, tap % 3
@@ -181,6 +169,38 @@
         for c in copies:
             c.start()
 
+        for c in copies:
+            c.wait()
+
+    return pl.pallas_call(
+        kernel,
+        in_specs=[pl.BlockSpec(memory_space=pl.ANY), pl.BlockSpec(memory_space=pltpu.HBM)],
+        out_specs=pl.BlockSpec(memory_space=pltpu.VMEM),
+        out_shape=jax.ShapeDtypeStruct((9 * channels, out_channels), BF16),
+        scratch_shapes=[pltpu.SemaphoreType.DMA((18,))],
+        compiler_params=pltpu.CompilerParams(vmem_limit_bytes=50 * 2**20),
+        cost_estimate=pl.CostEstimate(flops=5 * 10**9, bytes_accessed=0, transcendentals=0),
+        name="conv_weights",
+    )
+
+
+def make_main(rows, cols, channels, out_channels, tile_rows, count):
+    per_group = channels // NORM_GROUPS
+    rim = OVER // 2
+    rim_blocks = rim // cols
+    stride_blocks = STRIDE // cols
+    tile_blocks = TILE // cols
+    pixels = rows * cols
+    main = (channels // 128) * 128
+    rem = channels - main
+    depth = 9 * channels
+    sub_items = float((rows // DIL) * (cols // DIL) * count * per_group)
+    all_rows = 32 + tile_rows
+
+    def kernel(
+        x_ref, ha_ref, hb_ref, stats_ref, vec_ref, bw_ref, w_ref, o_ref,
+        a_ref, sub_ref, blend_ref, sc_ref, sh_ref, tsc_ref, tsh_ref,
+    ):
         block = lax.axis_index("wide")
         even = lax.rem(block, 2) == 0
         tile0 = lax.div(block + rim_blocks, stride_blocks)
@@ -230,19 +250,12 @@
         left_ok = jnp.where(block > 0, 1.0, 0.0).astype(F32)
         right_ok = jnp.where(block < count - 1, 1.0, 0.0).astype(F32)
 
-        for r in range(DIL):
-            sub_ref[r] = jnp.zeros((4 * 8, channels), F32)
-            sub_ref[rows + DIL + r] = jnp.zeros((4 * 8, channels), F32)
-        for j in range(3):
-            blend_ref[j, 0] = jnp.zeros((cols, channels), F32)
-            blend_ref[j, rows + 1] = jnp.zeros((cols, channels), F32)
-
         sub_id = iota((8, channels), 0)
         def silu(x, scale, offset):
             h = x * scale + offset
             return h + h * jnp.tanh(h)
 
-        def activate(m, carry):
+        def activate(m, tiles):
             ha = ha_ref[pl.ds(pl.multiple_of(16 * m, 16), 16), :].astype(F32)
             hb = hb_ref[pl.ds(pl.multiple_of(16 * m, 16), 16), :].astype(F32)
             left = jnp.where(even, hb, ha)
@@ -255,39 +268,66 @@
                 res = pl.multiple_of(lax.rem(r, DIL) * 8, 8)
                 scale = sc_ref[pl.ds(res, 8), :]
                 offset = sh_ref[pl.ds(res, 8), :]
-                sub_ref[r + DIL, 0:8, :] = silu(xl, scale, offset) * left_ok
-                sub_ref[r + DIL, 8:16, :] = silu(x0, scale, offset)
-                sub_ref[r + DIL, 16:24, :] = silu(x1, scale, offset)
-                sub_ref[r + DIL, 24:32, :] = silu(xr, scale, offset) * right_ok
+                sub_ref[r, 0:8, :] = silu(xl, scale, offset) * left_ok
+                sub_ref[r, 8:16, :] = silu(x0, scale, offset)
+                sub_ref[r, 16:24, :] = silu(x1, scale, offset)
+                sub_ref[r, 24:32, :] = silu(xr, scale, offset) * right_ok
                 xh = jnp.where(sub_id < 4, xr, xl)
                 acts = [
-                    [silu(v, tsc_ref[8 * t : 8 * t + 8, :], tsh_ref[8 * t : 8 * t + 8, :]) for t in range(2)]
+                    [
+                        silu(v, tsc_ref[8 * t : 8 * t + 8, :], tsh_ref[8 * t : 8 * t + 8, :])
+                        for t in range(tiles)
+                    ]
                     for v in (x0, x1, xh)
                 ]
 
                 def mix(j, k):
+                    if tiles == 1:
+                        return acts[k][0] if k < 2 else acts[k][0] * rim_ok
                     return bw_ref[j, k, 0] * acts[k][0] + bw_ref[j, k, 1] * acts[k][1]
 
-                blend_ref[1, r + 1, 0:8, :] = mix(1, 0)
-                blend_ref[1, r + 1, 8:16, :] = mix(1, 1)
+                blend_ref[1, r, 0:8, :] = mix(1, 0)
+                blend_ref[1, r, 8:16, :] = mix(1, 1)
                 f = [pltpu.roll(mix(2, k), 7, 0) for k in range(3)]
-                blend_ref[2, r + 1, 0:8, :] = jnp.where(sub_id < 7, f[0], f[1])
-                blend_ref[2, r + 1, 8:16, :] = jnp.where(sub_id < 7, f[1], f[2])
+                blend_ref[2, r, 0:8, :] = jnp.where(sub_id < 7, f[0], f[1])
+                blend_ref[2, r, 8:16, :] = jnp.where(sub_id < 7, f[1], f[2])
                 g = [pltpu.roll(mix(0, k), 1, 0) for k in range(3)]
-                blend_ref[0, r + 1, 0:8, :] = jnp.where(sub_id > 0, g[0], g[2])
-                blend_ref[0, r + 1, 8:16, :] = jnp.where(sub_id > 0, g[1], g[0])
-            return carry
-
-        lax.fori_loop(0, rows // 2, activate, 0)
-
-        def gather(r, carry):
-            at = pl.ds(pl.multiple_of(r * cols, cols), cols)
+                blend_ref[0, r, 0:8, :] = jnp.where(sub_id > 0, g[0], g[2])
+                blend_ref[0, r, 8:16, :] = jnp.where(sub_id > 0, g[1], g[0])
+
+        rim_col = jnp.where(sub_id < 4, sub_id + cols, sub_id - 8) + block * cols
+        rim_at = rim_col - (tile0 * STRIDE - rim)
+        rim_in = (rim_at >= 0) & (rim_at < TILE) & (rim_col >= 0) & (rim_col < count * cols)
+        rim_ok = jnp.where(rim_in, 1.0, 0.0).astype(F32)
+        shared = (tile1 >= 0) & (block < tile1 * stride_blocks - rim_blocks + tile_blocks)
+
+        @pl.when(shared)
+        def _():
+            @pl.loop(0, rows // 2, unroll=2)
+            def _(m):
+                activate(m, 2)
+
+        @pl.when(jnp.logical_not(shared))
+        def _():
+            @pl.loop(0, rows // 2, unroll=2)
+            def _(m):
+                activate(m, 1)
+
+        def gather(r):
+            at = pl.ds(r * cols, cols)
             held = None
             for tap in range(9):
                 i, j = tap // 3, tap % 3
-                v = (
-                    blend_ref[j, r + i] + sub_ref[r + DIL * i, 8 * j : 8 * j + cols, :]
-                ).astype(BF16)
+                near, far = r + i - 1, r + DIL * (i - 1)
+                v = None
+                if 0 <= near < rows:
+                    v = blend_ref[j, near]
+                if 0 <= far < rows:
+                    w = sub_ref[far, 8 * j : 8 * j + cols, :]
+                    v = w if v is None else v + w
+                if v is None:
+                    v = jnp.zeros((cols, channels), F32)
+                v = v.astype(BF16)
                 a_ref[at, tap * main : (tap + 1) * main] = v[:, :main]
                 if rem:
                     base = 9 * main + tap * rem
@@ -299,13 +339,10 @@
                         )
                     else:
                         a_ref[at, base : base + rem] = v[:, main:]
-            return carry
-
-        for c in copies:
-            c.wait()
+
         for m in range(0, rows, 8):
             for r in range(m, m + 8):
-                gather(r, 0)
+                gather(r)
             at = pl.ds(m * cols, 8 * cols)
             acc = jnp.dot(a_ref[at, :], w_ref[...], preferred_element_type=F32)
             o_ref[at, :] = (0.5 * acc + bias).astype(BF16)
@@ -313,21 +350,19 @@
     vmem = pl.BlockSpec(memory_space=pltpu.VMEM)
     return pl.pallas_call(
         kernel,
-        in_specs=[vmem] * 6 + [pl.BlockSpec(memory_space=pltpu.HBM)],
+        in_specs=[vmem] * 7,
         out_specs=vmem,
         out_shape=jax.ShapeDtypeStruct((pixels, out_channels), BF16),
         scratch_shapes=[
-            pltpu.VMEM((depth, out_channels), BF16),
-            pltpu.SemaphoreType.DMA((18,)),
             pltpu.VMEM((pixels, depth), BF16),
-            pltpu.VMEM((rows + 2 * DIL, 4 * 8, channels), F32),
-            pltpu.VMEM((3, rows + 2, cols, channels), F32),
+            pltpu.VMEM((rows, 4 * 8, channels), F32),
+            pltpu.VMEM((3, rows, cols, channels), F32),
             pltpu.VMEM((64, channels), F32),
             pltpu.VMEM((64, channels), F32),
             pltpu.VMEM((16, channels), F32),
             pltpu.VMEM((16, channels), F32),
         ],
-        compiler_params=pltpu.CompilerParams(vmem_limit_bytes=52 * 2**20),
+        compiler_params=pltpu.CompilerParams(vmem_limit_bytes=40 * 2**20),
         name="norm_conv",
     )
 
@@ -352,6 +387,7 @@
 
         spare = jnp.zeros((-channels % 128,), F32)
         vectors = jnp.concatenate([gain, spare, shift, spare, bias, spare])
+        taps = None
         step = 1
         while step < count:
             stats = summed(stats, step)
@@ -362,8 +398,12 @@
                 halo_b = lax.ppermute(edge_b, "wide", pairs_b)
                 blend = make_blend(cols, channels, count)(stats)
             step *= 2
+            if step == 4 or (taps is None and step >= count):
+                taps = make_weights(channels, out_channels)(stats, weight)
+            if step == 8:
+                taps, stats = lax.optimization_barrier((taps, stats))
         out = make_main(rows, cols, channels, out_channels, tile_rows, count)(
-            x_near, halo_a, halo_b, stats, vectors, blend, weight
+            x_near, halo_a, halo_b, stats, vectors, blend, taps
         )
         return out.reshape(rows, cols, out_channels)
 

time: 23 us -> 22.4 us (0.974)
  waiting for transfers between devices: 7.5 us -> 5.67 us
  Pallas kernels: 5.38 us -> 6.62 us
    ppermute x4, waiting for transfers between devices: 7.5 us -> 5.66 us  [summed(): lax.ppermute(stats, 'wide', [(i, i ^ step) for i in range(count)])]
    pallas_call x0 -> x1, Pallas kernels: none -> 1.81 us  [local(): taps = make_weights(channels, out_channels)(stats, weight)]
    pallas_call x1, Pallas kernels: 4.56 us -> 3.76 us  [local(): make_main(rows, cols, channels, out_channels, tile_rows, count)]
  transfers between devices with their start and end apart: 6 -> 6, of which waited for: 4 -> 4; matrix products, arithmetic and copies ran while one was open for 0% -> 0% of each run, Pallas kernels for 0% -> 8%
where the time goes in v4:
time: 22.4 us; the launch traced here: 22.2 us
  starting transfers between devices  8.79 us (39%)
  Pallas kernels  6.62 us (30%)
  waiting for transfers between devices  5.67 us (25%)
  local copies, waits for them, and re-layouts  1.09 us (5%)
    ppermute x4, starting transfers between devices, summed(): lax.ppermute(stats, 'wide', [(i, i ^ step) for i in range(count)])  8.06 us
    ppermute x4, waiting for transfers between devices, summed(): lax.ppermute(stats, 'wide', [(i, i ^ step) for i in range(count)])  5.66 us
    pallas_call x1, Pallas kernels, local(): make_main(rows, cols, channels, out_channels, tile_rows, count)  3.76 us
    pallas_call x1, Pallas kernels, local(): taps = make_weights(channels, out_channels)(stats, weight)  1.81 us
    unnamed x8, local copies, waits for them, and re-layouts  1.01 us
    pallas_call x1, Pallas kernels, local(): make_stats(rows, cols, channels, tile_rows)(x)  0.98 us
    ppermute x1, starting transfers between devices, local(): halo_b = lax.ppermute(edge_b, 'wide', pairs_b)  0.67 us
  transfers between devices with their start and end apart: 6, of which 4 were waited for; matrix products, arithmetic and copies ran while one was open for 0% of the time, Pallas kernels for 8%

profile of v4, /device:TPU:0, one launch (start us, length us, event | category | flops | bytes accessed | tf_op | source)
XLA Modules:
  0.0 22.2 jit_solution(2075251954918221815)
XLA Ops:
  0.0 0.0 copy-start
  0.0 1.0 %copy-done = bf16[32,16,320]{2,1,0:T(8,128)(2,1)S(1)} copy-done((bf16[32,16,320]{2,1,0:T(8,128)(2,1)S(1)}, bf16[32,16,320]{2,1,0:T(8,128)(2,1)}, u32[]{:S(2)}) %copy-start) | copy-done | bytes 327704
  1.0 1.0 %block_stats.1 = (f32[40,128]{1,0:T(8,128)S(1)}, bf16[256,320]{1,0:T(8,128)(2,1)}, bf16[256,320]{1,0:T(8,128)(2,1)S(1)}, bf16[512,320]{1,0:T(8,128)(2,1)S(1)}) custom-call(bf16[512,320]{1,0:T(8,128)(2,1)S(1)} %bitcast.2), custom_call_target="tpu_custom_call" | custom-call | tf_op jit(solution)/shard_map/block_stats/pallas_call | solution.py:378
  2.0 0.5 %collective-permute-start.1 = (f32[40,128]{1,0:T(8,128)S(1)}, f32[40,128]{1,0:T(8,128)S(1)}, u32[]{:S(2)}, u32[]{:S(2)}) collective-permute-start(f32[40,128]{1,0:T(8,128)S(1)} %get-tuple-element.18), channel_id=1, source_target_pairs={{0,1},{1,0},{2,3},{3,2},{4,5},{5,4},{6,7},{7,6},{8,9},{9,8},{10,11... | collective-permute-start | bytes 61448 | tf_op jit(solution)/shard_map/ppermute | solution.py:386
  2.4 0.1 collective-permute-start
  2.5 0.8 %collective-permute-done.1 = f32[40,128]{1,0:T(8,128)S(1)} collective-permute-done((f32[40,128]{1,0:T(8,128)S(1)}, f32[40,128]{1,0:T(8,128)S(1)}, u32[]{:S(2)}, u32[]{:S(2)}) %collective-permute-start.1) | collective-permute-done | bytes 20512 | tf_op jit(solution)/shard_map/ppermute | solution.py:386
  3.3 2.9 %collective-permute-start.3 = (f32[40,128]{1,0:T(8,128)S(1)}, f32[40,128]{1,0:T(8,128)S(1)}, u32[]{:S(2)}, u32[]{:S(2)}) collective-permute-start(f32[40,128]{1,0:T(8,128)S(1)} %add.12.after_ref), channel_id=1, source_target_pairs={{0,2},{1,3},{2,0},{3,1},{4,6},{5,7},{6,4},{7,5},{8,10},{9,11},{10,... | collective-permute-start | bytes 61448 | tf_op jit(solution)/shard_map/ppermute | solution.py:386
  6.1 0.1 blend_weights.1.bw_ref
  6.2 0.7 %collective-permute-start.2 = (bf16[256,320]{1,0:T(8,128)(2,1)S(1)}, bf16[256,320]{1,0:T(8,128)(2,1)S(1)}, u32[]{:S(2)}, u32[]{:S(2)}) collective-permute-start(bf16[256,320]{1,0:T(8,128)(2,1)S(1)} %get-tuple-element.19), channel_id=1, source_target_pairs={{1,2},{2,1},{3,4},{4,3},{5,6},{6,5},{7,8},{8,7},{9,10},{10,9},{11,... | collective-permute-start | bytes 491528 | tf_op jit(solution)/shard_map/ppermute | solution.py:398
  6.9 1.0 %collective-permute-done.3 = f32[40,128]{1,0:T(8,128)S(1)} collective-permute-done((f32[40,128]{1,0:T(8,128)S(1)}, f32[40,128]{1,0:T(8,128)S(1)}, u32[]{:S(2)}, u32[]{:S(2)}) %collective-permute-start.3) | collective-permute-done | bytes 20512 | tf_op jit(solution)/shard_map/ppermute | solution.py:386
  7.9 0.0 copy-start.1
  7.9 0.0 copy-start.2
  7.9 0.0 copy-start.3
  7.9 2.2 %collective-permute-start.4 = (f32[40,128]{1,0:T(8,128)S(1)}, f32[40,128]{1,0:T(8,128)S(1)}, u32[]{:S(2)}, u32[]{:S(2)}) collective-permute-start(f32[40,128]{1,0:T(8,128)S(1)} %add.13.after_ref), channel_id=1, source_target_pairs={{0,4},{1,5},{2,6},{3,7},{4,0},{5,1},{6,2},{7,3},{8,12},{9,13},{10,... | collective-permute-start | bytes 61448 | tf_op jit(solution)/shard_map/ppermute | solution.py:386
  10.1 1.8 %conv_weights.1.w_ref = bf16[2880,320]{1,0:T(8,128)(2,1)S(1)} custom-call(f32[40,128]{1,0:T(8,128)S(1)} %add.13.after_ref, bf16[3,3,320,320]{3,2,1,0:T(8,128)(2,1)} %w_hbm.1), custom_call_target="tpu_custom_call" | custom-call | flops 5000000000 | tf_op jit(solution)/shard_map/conv_weights/pallas_call | solution.py:402
  11.9 1.9 %collective-permute-done.4 = f32[40,128]{1,0:T(8,128)S(1)} collective-permute-done((f32[40,128]{1,0:T(8,128)S(1)}, f32[40,128]{1,0:T(8,128)S(1)}, u32[]{:S(2)}, u32[]{:S(2)}) %collective-permute-start.4) | collective-permute-done | bytes 20512 | tf_op jit(solution)/shard_map/ppermute | solution.py:386
  13.8 2.6 %collective-permute-start.5 = (f32[40,128]{1,0:T(8,128)S(1)}, f32[40,128]{1,0:T(8,128)S(1)}, u32[]{:S(2)}, u32[]{:S(2)}) collective-permute-start(f32[40,128]{1,0:T(8,128)S(1)} %add.14), channel_id=1, source_target_pairs={{0,8},{1,9},{2,10},{3,11},{4,12},{5,13},{6,14},{7,15},{8,0},{9,1},... | collective-permute-start | bytes 61448 | tf_op jit(solution)/shard_map/ppermute | solution.py:386
  16.4 0.0 copy-done.1
  16.4 0.0 copy-done.2
  16.4 0.0 copy-done.3
  16.4 0.1 concatenate.3.vec_ref
  16.5 2.0 %collective-permute-done.5 = f32[40,128]{1,0:T(8,128)S(1)} collective-permute-done((f32[40,128]{1,0:T(8,128)S(1)}, f32[40,128]{1,0:T(8,128)S(1)}, u32[]{:S(2)}, u32[]{:S(2)}) %collective-permute-start.5) | collective-permute-done | bytes 20512 | tf_op jit(solution)/shard_map/ppermute | solution.py:386
  18.5 0.0 collective-permute-done.ha_ref
  18.5 0.0 collective-permute-done.2.hb_ref
  18.5 3.8 %norm_conv.1 = bf16[512,320]{1,0:T(8,128)(2,1)} custom-call(bf16[512,320]{1,0:T(8,128)(2,1)S(1)} %get-tuple-element.15.x_ref, bf16[256,320]{1,0:T(8,128)(2,1)S(1)} %collective-permute-done.ha_ref, bf16[256,320]{1,0:T(8,128)(2,1)S(1)} %collective-permute-done.2.hb_ref, f32[40,128]{1,0:T(8,128)S(1)} %add.15.stats_ref, f32[1152]{0:T(1024)S(1)} %concatenate.3.vec_ref, ...), custom_call_target="tpu_custom_call" | custom-call | tf_op jit(solution)/shard_map/norm_conv/pallas_call | solution.py:405
  (5 shorter events, 0.0 us)
Async XLA Ops:
  0.0 1.0 %copy-start = (bf16[32,16,320]{2,1,0:T(8,128)(2,1)S(1)}, bf16[32,16,320]{2,1,0:T(8,128)(2,1)}, u32[]{:S(2)}) copy-start(bf16[32,16,320]{2,1,0:T(8,128)(2,1)} %param.5) | copy-start | bytes 983044
  2.0 1.3 %collective-permute-start.1 = (f32[40,128]{1,0:T(8,128)S(1)}, f32[40,128]{1,0:T(8,128)S(1)}, u32[]{:S(2)}, u32[]{:S(2)}) collective-permute-start(f32[40,128]{1,0:T(8,128)S(1)} %get-tuple-element.18), channel_id=1, source_target_pairs={{0,1},{1,0},{2,3},{3,2},{4,5},{5,4},{6,7},{7,6},{8,9},{9,8},{10,11... | collective-permute-start | bytes 61448 | tf_op jit(solution)/shard_map/ppermute | solution.py:386
  2.4 16.0 %collective-permute-start = (bf16[256,320]{1,0:T(8,128)(2,1)}, bf16[256,320]{1,0:T(8,128)(2,1)S(1)}, u32[]{:S(2)}, u32[]{:S(2)}) collective-permute-start(bf16[256,320]{1,0:T(8,128)(2,1)} %get-tuple-element.16), channel_id=1, source_target_pairs={{0,1},{1,0},{2,3},{3,2},{4,5},{5,4},{6,7},{7,6},{8,9},{9,8},{10,11... | collective-permute-start | bytes 491528 | tf_op jit(solution)/shard_map/ppermute | solution.py:383
  3.3 4.6 %collective-permute-start.3 = (f32[40,128]{1,0:T(8,128)S(1)}, f32[40,128]{1,0:T(8,128)S(1)}, u32[]{:S(2)}, u32[]{:S(2)}) collective-permute-start(f32[40,128]{1,0:T(8,128)S(1)} %add.12.after_ref), channel_id=1, source_target_pairs={{0,2},{1,3},{2,0},{3,1},{4,6},{5,7},{6,4},{7,5},{8,10},{9,11},{10,... | collective-permute-start | bytes 61448 | tf_op jit(solution)/shard_map/ppermute | solution.py:386
  6.2 12.3 %collective-permute-start.2 = (bf16[256,320]{1,0:T(8,128)(2,1)S(1)}, bf16[256,320]{1,0:T(8,128)(2,1)S(1)}, u32[]{:S(2)}, u32[]{:S(2)}) collective-permute-start(bf16[256,320]{1,0:T(8,128)(2,1)S(1)} %get-tuple-element.19), channel_id=1, source_target_pairs={{1,2},{2,1},{3,4},{4,3},{5,6},{6,5},{7,8},{8,7},{9,10},{10,9},{11,... | collective-permute-start | bytes 491528 | tf_op jit(solution)/shard_map/ppermute | solution.py:398
  7.9 8.5 %copy-start.1 = (f32[320]{0:T(512)S(1)}, f32[320]{0:T(512)}, u32[]{:S(2)}) copy-start(f32[320]{0:T(512)} %param.6) | copy-start | bytes 3844
  7.9 8.5 %copy-start.2 = (f32[320]{0:T(512)S(1)}, f32[320]{0:T(512)}, u32[]{:S(2)}) copy-start(f32[320]{0:T(512)} %param.7) | copy-start | bytes 3844
  7.9 8.5 %copy-start.3 = (f32[320]{0:T(512)S(1)}, f32[320]{0:T(512)}, u32[]{:S(2)}) copy-start(f32[320]{0:T(512)} %param.9) | copy-start | bytes 3844
  7.9 5.8 %collective-permute-start.4 = (f32[40,128]{1,0:T(8,128)S(1)}, f32[40,128]{1,0:T(8,128)S(1)}, u32[]{:S(2)}, u32[]{:S(2)}) collective-permute-start(f32[40,128]{1,0:T(8,128)S(1)} %add.13.after_ref), channel_id=1, source_target_pairs={{0,4},{1,5},{2,6},{3,7},{4,0},{5,1},{6,2},{7,3},{8,12},{9,13},{10,... | collective-permute-start | bytes 61448 | tf_op jit(solution)/shard_map/ppermute | solution.py:386
  13.8 4.7 %collective-permute-start.5 = (f32[40,128]{1,0:T(8,128)S(1)}, f32[40,128]{1,0:T(8,128)S(1)}, u32[]{:S(2)}, u32[]{:S(2)}) collective-permute-start(f32[40,128]{1,0:T(8,128)S(1)} %add.14), channel_id=1, source_target_pairs={{0,8},{1,9},{2,10},{3,11},{4,12},{5,13},{6,14},{7,15},{8,0},{9,1},... | collective-permute-start | bytes 61448 | tf_op jit(solution)/shard_map/ppermute | solution.py:386

commit v5 on v4

--- a/solution.py
+++ b/solution.py
@@ -383,7 +383,8 @@
         halo_a = lax.ppermute(edge_a, "wide", pairs_a)
 
         def summed(stats, step):
-            return stats + lax.ppermute(stats, "wide", [(i, i ^ step) for i in range(count)])
+            mask = step + 1 if 1 < step < 8 else step
+            return stats + lax.ppermute(stats, "wide", [(i, i ^ mask) for i in range(count)])
 
         spare = jnp.zeros((-channels % 128,), F32)
         vectors = jnp.concatenate([gain, spare, shift, spare, bias, spare])

time: 22.4 us -> 21.1 us (0.942)
  the two profiles are of different devices: /device:TPU:0 before, /device:TPU:14 now
where the time goes in v5:
time: 21.1 us; the launch traced here: 20.9 us
  starting transfers between devices  8 us (38%)
  Pallas kernels  7.15 us (34%)
  waiting for transfers between devices  4.6 us (22%)
  local copies, waits for them, and re-layouts  1.1 us (5%)
    ppermute x4, waiting for transfers between devices, summed(): lax.ppermute(stats, 'wide', [(i, i ^ mask) for i in range(count)])  4.59 us
    pallas_call x1, Pallas kernels, local(): make_main(rows, cols, channels, out_channels, tile_rows, count)  4.3 us
    ppermute x4, starting transfers between devices, summed(): lax.ppermute(stats, 'wide', [(i, i ^ mask) for i in range(count)])  4.12 us
    ppermute x1, starting transfers between devices, local(): halo_b = lax.ppermute(edge_b, 'wide', pairs_b)  3.38 us
    pallas_call x1, Pallas kernels, local(): taps = make_weights(channels, out_channels)(stats, weight)  1.81 us
    unnamed x8, local copies, waits for them, and re-layouts  1.01 us
    pallas_call x1, Pallas kernels, local(): make_stats(rows, cols, channels, tile_rows)(x)  0.98 us
    ppermute x1, starting transfers between devices, local(): halo_a = lax.ppermute(edge_a, 'wide', pairs_a)  0.51 us
  transfers between devices with their start and end apart: 6, of which 3 were waited for; matrix products, arithmetic and copies ran while one was open for 0% of the time, Pallas kernels for 9%

profile of v5, /device:TPU:14, one launch (start us, length us, event | category | flops | bytes accessed | tf_op | source)
XLA Modules:
  0.0 20.9 jit_solution(11638010734868522587)
XLA Ops:
  0.0 0.0 copy-start
  0.0 1.0 %copy-done = bf16[32,16,320]{2,1,0:T(8,128)(2,1)S(1)} copy-done((bf16[32,16,320]{2,1,0:T(8,128)(2,1)S(1)}, bf16[32,16,320]{2,1,0:T(8,128)(2,1)}, u32[]{:S(2)}) %copy-start) | copy-done | bytes 327704
  1.0 1.0 %block_stats.1 = (f32[40,128]{1,0:T(8,128)S(1)}, bf16[256,320]{1,0:T(8,128)(2,1)}, bf16[256,320]{1,0:T(8,128)(2,1)S(1)}, bf16[512,320]{1,0:T(8,128)(2,1)S(1)}) custom-call(bf16[512,320]{1,0:T(8,128)(2,1)S(1)} %bitcast.2), custom_call_target="tpu_custom_call" | custom-call | tf_op jit(solution)/shard_map/block_stats/pallas_call | solution.py:378
  2.0 0.0 collective-permute-start.1
  2.0 0.5 %collective-permute-start = (bf16[256,320]{1,0:T(8,128)(2,1)}, bf16[256,320]{1,0:T(8,128)(2,1)S(1)}, u32[]{:S(2)}, u32[]{:S(2)}) collective-permute-start(bf16[256,320]{1,0:T(8,128)(2,1)} %get-tuple-element.16), channel_id=1, source_target_pairs={{0,1},{1,0},{2,3},{3,2},{4,5},{5,4},{6,7},{7,6},{8,9},{9,8},{10,11... | collective-permute-start | bytes 491528 | tf_op jit(solution)/shard_map/ppermute | solution.py:383
  2.5 0.7 %collective-permute-done.1 = f32[40,128]{1,0:T(8,128)S(1)} collective-permute-done((f32[40,128]{1,0:T(8,128)S(1)}, f32[40,128]{1,0:T(8,128)S(1)}, u32[]{:S(2)}, u32[]{:S(2)}) %collective-permute-start.1) | collective-permute-done | bytes 20512 | tf_op jit(solution)/shard_map/ppermute | solution.py:387
  3.2 0.3 %collective-permute-start.3 = (f32[40,128]{1,0:T(8,128)S(1)}, f32[40,128]{1,0:T(8,128)S(1)}, u32[]{:S(2)}, u32[]{:S(2)}) collective-permute-start(f32[40,128]{1,0:T(8,128)S(1)} %add.12.after_ref), channel_id=1, source_target_pairs={{0,3},{1,2},{2,1},{3,0},{4,7},{5,6},{6,5},{7,4},{8,11},{9,10},{10,... | collective-permute-start | bytes 61448 | tf_op jit(solution)/shard_map/ppermute | solution.py:387
  3.5 0.1 blend_weights.1.bw_ref
  3.5 3.4 %collective-permute-start.2 = (bf16[256,320]{1,0:T(8,128)(2,1)S(1)}, bf16[256,320]{1,0:T(8,128)(2,1)S(1)}, u32[]{:S(2)}, u32[]{:S(2)}) collective-permute-start(bf16[256,320]{1,0:T(8,128)(2,1)S(1)} %get-tuple-element.19), channel_id=1, source_target_pairs={{1,2},{2,1},{3,4},{4,3},{5,6},{6,5},{7,8},{8,7},{9,10},{10,9},{11,... | collective-permute-start | bytes 491528 | tf_op jit(solution)/shard_map/ppermute | solution.py:399
  6.9 0.0 collective-permute-done.3
  6.9 0.0 copy-start.1
  6.9 0.0 copy-start.2
  6.9 0.0 copy-start.3
  7.0 1.3 %collective-permute-start.4 = (f32[40,128]{1,0:T(8,128)S(1)}, f32[40,128]{1,0:T(8,128)S(1)}, u32[]{:S(2)}, u32[]{:S(2)}) collective-permute-start(f32[40,128]{1,0:T(8,128)S(1)} %add.13.after_ref), channel_id=1, source_target_pairs={{0,5},{1,4},{2,7},{3,6},{4,1},{5,0},{6,3},{7,2},{8,13},{9,12},{10,... | collective-permute-start | bytes 61448 | tf_op jit(solution)/shard_map/ppermute | solution.py:387
  8.3 1.8 %conv_weights.1.w_ref = bf16[2880,320]{1,0:T(8,128)(2,1)S(1)} custom-call(f32[40,128]{1,0:T(8,128)S(1)} %add.13.after_ref, bf16[3,3,320,320]{3,2,1,0:T(8,128)(2,1)} %w_hbm.1), custom_call_target="tpu_custom_call" | custom-call | flops 5000000000 | tf_op jit(solution)/shard_map/conv_weights/pallas_call | solution.py:403
  10.1 1.9 %collective-permute-done.4 = f32[40,128]{1,0:T(8,128)S(1)} collective-permute-done((f32[40,128]{1,0:T(8,128)S(1)}, f32[40,128]{1,0:T(8,128)S(1)}, u32[]{:S(2)}, u32[]{:S(2)}) %collective-permute-start.4) | collective-permute-done | bytes 20512 | tf_op jit(solution)/shard_map/ppermute | solution.py:387
  11.9 2.5 %collective-permute-start.5 = (f32[40,128]{1,0:T(8,128)S(1)}, f32[40,128]{1,0:T(8,128)S(1)}, u32[]{:S(2)}, u32[]{:S(2)}) collective-permute-start(f32[40,128]{1,0:T(8,128)S(1)} %add.14), channel_id=1, source_target_pairs={{0,8},{1,9},{2,10},{3,11},{4,12},{5,13},{6,14},{7,15},{8,0},{9,1},... | collective-permute-start | bytes 61448 | tf_op jit(solution)/shard_map/ppermute | solution.py:387
  14.5 0.0 copy-done.1
  14.5 0.0 copy-done.2
  14.5 0.0 copy-done.3
  14.5 0.1 concatenate.3.vec_ref
  14.6 2.0 %collective-permute-done.5 = f32[40,128]{1,0:T(8,128)S(1)} collective-permute-done((f32[40,128]{1,0:T(8,128)S(1)}, f32[40,128]{1,0:T(8,128)S(1)}, u32[]{:S(2)}, u32[]{:S(2)}) %collective-permute-start.5) | collective-permute-done | bytes 20512 | tf_op jit(solution)/shard_map/ppermute | solution.py:387
  16.6 0.0 collective-permute-done.ha_ref
  16.6 0.0 collective-permute-done.2.hb_ref
  16.6 4.3 %norm_conv.1 = bf16[512,320]{1,0:T(8,128)(2,1)} custom-call(bf16[512,320]{1,0:T(8,128)(2,1)S(1)} %get-tuple-element.15.x_ref, bf16[256,320]{1,0:T(8,128)(2,1)S(1)} %collective-permute-done.ha_ref, bf16[256,320]{1,0:T(8,128)(2,1)S(1)} %collective-permute-done.2.hb_ref, f32[40,128]{1,0:T(8,128)S(1)} %add.15.stats_ref, f32[1152]{0:T(1024)S(1)} %concatenate.3.vec_ref, ...), custom_call_target="tpu_custom_call" | custom-call | tf_op jit(solution)/shard_map/norm_conv/pallas_call | solution.py:406
  (5 shorter events, 0.0 us)
Async XLA Ops:
  0.0 1.0 %copy-start = (bf16[32,16,320]{2,1,0:T(8,128)(2,1)S(1)}, bf16[32,16,320]{2,1,0:T(8,128)(2,1)}, u32[]{:S(2)}) copy-start(bf16[32,16,320]{2,1,0:T(8,128)(2,1)} %param.5) | copy-start | bytes 983044
  2.0 1.2 %collective-permute-start.1 = (f32[40,128]{1,0:T(8,128)S(1)}, f32[40,128]{1,0:T(8,128)S(1)}, u32[]{:S(2)}, u32[]{:S(2)}) collective-permute-start(f32[40,128]{1,0:T(8,128)S(1)} %get-tuple-element.18), channel_id=1, source_target_pairs={{0,1},{1,0},{2,3},{3,2},{4,5},{5,4},{6,7},{7,6},{8,9},{9,8},{10,11... | collective-permute-start | bytes 61448 | tf_op jit(solution)/shard_map/ppermute | solution.py:387
  2.0 14.7 %collective-permute-start = (bf16[256,320]{1,0:T(8,128)(2,1)}, bf16[256,320]{1,0:T(8,128)(2,1)S(1)}, u32[]{:S(2)}, u32[]{:S(2)}) collective-permute-start(bf16[256,320]{1,0:T(8,128)(2,1)} %get-tuple-element.16), channel_id=1, source_target_pairs={{0,1},{1,0},{2,3},{3,2},{4,5},{5,4},{6,7},{7,6},{8,9},{9,8},{10,11... | collective-permute-start | bytes 491528 | tf_op jit(solution)/shard_map/ppermute | solution.py:383
  3.2 3.7 %collective-permute-start.3 = (f32[40,128]{1,0:T(8,128)S(1)}, f32[40,128]{1,0:T(8,128)S(1)}, u32[]{:S(2)}, u32[]{:S(2)}) collective-permute-start(f32[40,128]{1,0:T(8,128)S(1)} %add.12.after_ref), channel_id=1, source_target_pairs={{0,3},{1,2},{2,1},{3,0},{4,7},{5,6},{6,5},{7,4},{8,11},{9,10},{10,... | collective-permute-start | bytes 61448 | tf_op jit(solution)/shard_map/ppermute | solution.py:387
  3.5 13.1 %collective-permute-start.2 = (bf16[256,320]{1,0:T(8,128)(2,1)S(1)}, bf16[256,320]{1,0:T(8,128)(2,1)S(1)}, u32[]{:S(2)}, u32[]{:S(2)}) collective-permute-start(bf16[256,320]{1,0:T(8,128)(2,1)S(1)} %get-tuple-element.19), channel_id=1, source_target_pairs={{1,2},{2,1},{3,4},{4,3},{5,6},{6,5},{7,8},{8,7},{9,10},{10,9},{11,... | collective-permute-start | bytes 491528 | tf_op jit(solution)/shard_map/ppermute | solution.py:399
  6.9 7.6 %copy-start.1 = (f32[320]{0:T(512)S(1)}, f32[320]{0:T(512)}, u32[]{:S(2)}) copy-start(f32[320]{0:T(512)} %param.6) | copy-start | bytes 3844
  6.9 7.6 %copy-start.2 = (f32[320]{0:T(512)S(1)}, f32[320]{0:T(512)}, u32[]{:S(2)}) copy-start(f32[320]{0:T(512)} %param.7) | copy-start | bytes 3844
  6.9 7.6 %copy-start.3 = (f32[320]{0:T(512)S(1)}, f32[320]{0:T(512)}, u32[]{:S(2)}) copy-start(f32[320]{0:T(512)} %param.9) | copy-start | bytes 3844
  7.0 5.0 %collective-permute-start.4 = (f32[40,128]{1,0:T(8,128)S(1)}, f32[40,128]{1,0:T(8,128)S(1)}, u32[]{:S(2)}, u32[]{:S(2)}) collective-permute-start(f32[40,128]{1,0:T(8,128)S(1)} %add.13.after_ref), channel_id=1, source_target_pairs={{0,5},{1,4},{2,7},{3,6},{4,1},{5,0},{6,3},{7,2},{8,13},{9,12},{10,... | collective-permute-start | bytes 61448 | tf_op jit(solution)/shard_map/ppermute | solution.py:387
  11.9 4.7 %collective-permute-start.5 = (f32[40,128]{1,0:T(8,128)S(1)}, f32[40,128]{1,0:T(8,128)S(1)}, u32[]{:S(2)}, u32[]{:S(2)}) collective-permute-start(f32[40,128]{1,0:T(8,128)S(1)} %add.14), channel_id=1, source_target_pairs={{0,8},{1,9},{2,10},{3,11},{4,12},{5,13},{6,14},{7,15},{8,0},{9,1},... | collective-permute-start | bytes 61448 | tf_op jit(solution)/shard_map/ppermute | solution.py:387

commit v6 on v5

--- a/solution.py
+++ b/solution.py
@@ -393,7 +393,7 @@
         while step < count:
             stats = summed(stats, step)
             if step == 2:
-                blend, stats = lax.optimization_barrier((blend, stats))
+                blend, halo_a, stats = lax.optimization_barrier((blend, halo_a, stats))
             if step == 1:
                 edge_b, stats = lax.optimization_barrier((edge_b, stats))
                 halo_b = lax.ppermute(edge_b, "wide", pairs_b)

time: 21.1 us -> 20.9 us (level)
  Pallas kernels: 7.15 us -> 6.92 us
    pallas_call x1, Pallas kernels: 0.98 us -> 0.75 us  [local(): make_stats(rows, cols, channels, tile_rows)(x)]
where the time goes in v6:
time: 20.9 us; the launch traced here: 20.7 us
  starting transfers between devices  8 us (38%)
  Pallas kernels  6.92 us (33%)
  waiting for transfers between devices  4.59 us (22%)
  local copies, waits for them, and re-layouts  1.1 us (5%)
    ppermute x4, waiting for transfers between devices, summed(): lax.ppermute(stats, 'wide', [(i, i ^ mask) for i in range(count)])  4.58 us
    pallas_call x1, Pallas kernels, local(): make_main(rows, cols, channels, out_channels, tile_rows, count)  4.3 us
    ppermute x4, starting transfers between devices, summed(): lax.ppermute(stats, 'wide', [(i, i ^ mask) for i in range(count)])  4.12 us
    ppermute x1, starting transfers between devices, local(): halo_b = lax.ppermute(edge_b, 'wide', pairs_b)  3.38 us
    pallas_call x1, Pallas kernels, local(): taps = make_weights(channels, out_channels)(stats, weight)  1.81 us
    unnamed x8, local copies, waits for them, and re-layouts  1.01 us
    pallas_call x1, Pallas kernels, local(): make_stats(rows, cols, channels, tile_rows)(x)  0.75 us
    ppermute x1, starting transfers between devices, local(): halo_a = lax.ppermute(edge_a, 'wide', pairs_a)  0.5 us
  transfers between devices with their start and end apart: 6, of which 3 were waited for; matrix products, arithmetic and copies ran while one was open for 0% of the time, Pallas kernels for 9%

profile of v6, /device:TPU:14, one launch (start us, length us, event | category | flops | bytes accessed | tf_op | source)
XLA Modules:
  0.0 20.7 jit_solution(1571199818544640423)
XLA Ops:
  0.0 0.0 copy-start
  0.0 1.0 %copy-done = bf16[32,16,320]{2,1,0:T(8,128)(2,1)S(1)} copy-done((bf16[32,16,320]{2,1,0:T(8,128)(2,1)S(1)}, bf16[32,16,320]{2,1,0:T(8,128)(2,1)}, u32[]{:S(2)}) %copy-start) | copy-done | bytes 327704
  1.0 0.8 %block_stats.1 = (f32[40,128]{1,0:T(8,128)S(1)}, bf16[256,320]{1,0:T(8,128)(2,1)S(1)}, bf16[256,320]{1,0:T(8,128)(2,1)S(1)}, bf16[512,320]{1,0:T(8,128)(2,1)S(1)}) custom-call(bf16[512,320]{1,0:T(8,128)(2,1)S(1)} %bitcast.2), custom_call_target="tpu_custom_call" | custom-call | tf_op jit(solution)/shard_map/block_stats/pallas_call | solution.py:378
  1.8 0.0 collective-permute-start
  1.8 0.5 %collective-permute-start.1 = (bf16[256,320]{1,0:T(8,128)(2,1)S(1)}, bf16[256,320]{1,0:T(8,128)(2,1)S(1)}, u32[]{:S(2)}, u32[]{:S(2)}) collective-permute-start(bf16[256,320]{1,0:T(8,128)(2,1)S(1)} %get-tuple-element.20), channel_id=1, source_target_pairs={{0,1},{1,0},{2,3},{3,2},{4,5},{5,4},{6,7},{7,6},{8,9},{9,8},{10,11... | collective-permute-start | bytes 491528 | tf_op jit(solution)/shard_map/ppermute | solution.py:383
  2.3 0.7 %collective-permute-done = f32[40,128]{1,0:T(8,128)S(1)} collective-permute-done((f32[40,128]{1,0:T(8,128)S(1)}, f32[40,128]{1,0:T(8,128)S(1)}, u32[]{:S(2)}, u32[]{:S(2)}) %collective-permute-start) | collective-permute-done | bytes 20512 | tf_op jit(solution)/shard_map/ppermute | solution.py:387
  3.0 0.3 %collective-permute-start.2 = (f32[40,128]{1,0:T(8,128)S(1)}, f32[40,128]{1,0:T(8,128)S(1)}, u32[]{:S(2)}, u32[]{:S(2)}) collective-permute-start(f32[40,128]{1,0:T(8,128)S(1)} %add.12.after_ref), channel_id=1, source_target_pairs={{0,3},{1,2},{2,1},{3,0},{4,7},{5,6},{6,5},{7,4},{8,11},{9,10},{10,... | collective-permute-start | bytes 61448 | tf_op jit(solution)/shard_map/ppermute | solution.py:387
  3.2 0.1 blend_weights.1.bw_ref
  3.3 3.4 %collective-permute-start.3 = (bf16[256,320]{1,0:T(8,128)(2,1)S(1)}, bf16[256,320]{1,0:T(8,128)(2,1)S(1)}, u32[]{:S(2)}, u32[]{:S(2)}) collective-permute-start(bf16[256,320]{1,0:T(8,128)(2,1)S(1)} %get-tuple-element.22), channel_id=1, source_target_pairs={{1,2},{2,1},{3,4},{4,3},{5,6},{6,5},{7,8},{8,7},{9,10},{10,9},{11,... | collective-permute-start | bytes 491528 | tf_op jit(solution)/shard_map/ppermute | solution.py:399
  6.7 0.0 collective-permute-done.2
  6.7 0.0 copy-start.1
  6.7 0.0 copy-start.2
  6.7 0.0 copy-start.3
  6.7 0.0 collective-permute-done.1.ha_ref
  6.7 1.3 %collective-permute-start.4 = (f32[40,128]{1,0:T(8,128)S(1)}, f32[40,128]{1,0:T(8,128)S(1)}, u32[]{:S(2)}, u32[]{:S(2)}) collective-permute-start(f32[40,128]{1,0:T(8,128)S(1)} %add.13.after_ref), channel_id=1, source_target_pairs={{0,5},{1,4},{2,7},{3,6},{4,1},{5,0},{6,3},{7,2},{8,13},{9,12},{10,... | collective-permute-start | bytes 61448 | tf_op jit(solution)/shard_map/ppermute | solution.py:387
  8.0 1.8 %conv_weights.1.w_ref = bf16[2880,320]{1,0:T(8,128)(2,1)S(1)} custom-call(f32[40,128]{1,0:T(8,128)S(1)} %add.13.after_ref, bf16[3,3,320,320]{3,2,1,0:T(8,128)(2,1)} %w_hbm.1), custom_call_target="tpu_custom_call" | custom-call | flops 5000000000 | tf_op jit(solution)/shard_map/conv_weights/pallas_call | solution.py:403
  9.9 1.9 %collective-permute-done.4 = f32[40,128]{1,0:T(8,128)S(1)} collective-permute-done((f32[40,128]{1,0:T(8,128)S(1)}, f32[40,128]{1,0:T(8,128)S(1)}, u32[]{:S(2)}, u32[]{:S(2)}) %collective-permute-start.4) | collective-permute-done | bytes 20512 | tf_op jit(solution)/shard_map/ppermute | solution.py:387
  11.7 2.5 %collective-permute-start.5 = (f32[40,128]{1,0:T(8,128)S(1)}, f32[40,128]{1,0:T(8,128)S(1)}, u32[]{:S(2)}, u32[]{:S(2)}) collective-permute-start(f32[40,128]{1,0:T(8,128)S(1)} %add.14), channel_id=1, source_target_pairs={{0,8},{1,9},{2,10},{3,11},{4,12},{5,13},{6,14},{7,15},{8,0},{9,1},... | collective-permute-start | bytes 61448 | tf_op jit(solution)/shard_map/ppermute | solution.py:387
  14.3 0.0 copy-done.1
  14.3 0.0 copy-done.2
  14.3 0.0 copy-done.3
  14.3 0.1 concatenate.3.vec_ref
  14.4 2.0 %collective-permute-done.5 = f32[40,128]{1,0:T(8,128)S(1)} collective-permute-done((f32[40,128]{1,0:T(8,128)S(1)}, f32[40,128]{1,0:T(8,128)S(1)}, u32[]{:S(2)}, u32[]{:S(2)}) %collective-permute-start.5) | collective-permute-done | bytes 20512 | tf_op jit(solution)/shard_map/ppermute | solution.py:387
  16.4 0.0 collective-permute-done.3.hb_ref
  16.4 4.3 %norm_conv.1 = bf16[512,320]{1,0:T(8,128)(2,1)} custom-call(bf16[512,320]{1,0:T(8,128)(2,1)S(1)} %get-tuple-element.16.x_ref, bf16[256,320]{1,0:T(8,128)(2,1)S(1)} %collective-permute-done.1.ha_ref, bf16[256,320]{1,0:T(8,128)(2,1)S(1)} %collective-permute-done.3.hb_ref, f32[40,128]{1,0:T(8,128)S(1)} %add.15.stats_ref, f32[1152]{0:T(1024)S(1)} %concatenate.3.vec_ref, ...), custom_call_target="tpu_custom_call" | custom-call | tf_op jit(solution)/shard_map/norm_conv/pallas_call | solution.py:406
  (5 shorter events, 0.0 us)
Async XLA Ops:
  0.0 1.0 %copy-start = (bf16[32,16,320]{2,1,0:T(8,128)(2,1)S(1)}, bf16[32,16,320]{2,1,0:T(8,128)(2,1)}, u32[]{:S(2)}) copy-start(bf16[32,16,320]{2,1,0:T(8,128)(2,1)} %param.5) | copy-start | bytes 983044
  1.8 1.2 %collective-permute-start = (f32[40,128]{1,0:T(8,128)S(1)}, f32[40,128]{1,0:T(8,128)S(1)}, u32[]{:S(2)}, u32[]{:S(2)}) collective-permute-start(f32[40,128]{1,0:T(8,128)S(1)} %get-tuple-element.18), channel_id=1, source_target_pairs={{0,1},{1,0},{2,3},{3,2},{4,5},{5,4},{6,7},{7,6},{8,9},{9,8},{10,11... | collective-permute-start | bytes 61448 | tf_op jit(solution)/shard_map/ppermute | solution.py:387
  1.8 5.0 %collective-permute-start.1 = (bf16[256,320]{1,0:T(8,128)(2,1)S(1)}, bf16[256,320]{1,0:T(8,128)(2,1)S(1)}, u32[]{:S(2)}, u32[]{:S(2)}) collective-permute-start(bf16[256,320]{1,0:T(8,128)(2,1)S(1)} %get-tuple-element.20), channel_id=1, source_target_pairs={{0,1},{1,0},{2,3},{3,2},{4,5},{5,4},{6,7},{7,6},{8,9},{9,8},{10,11... | collective-permute-start | bytes 491528 | tf_op jit(solution)/shard_map/ppermute | solution.py:383
  3.0 3.7 %collective-permute-start.2 = (f32[40,128]{1,0:T(8,128)S(1)}, f32[40,128]{1,0:T(8,128)S(1)}, u32[]{:S(2)}, u32[]{:S(2)}) collective-permute-start(f32[40,128]{1,0:T(8,128)S(1)} %add.12.after_ref), channel_id=1, source_target_pairs={{0,3},{1,2},{2,1},{3,0},{4,7},{5,6},{6,5},{7,4},{8,11},{9,10},{10,... | collective-permute-start | bytes 61448 | tf_op jit(solution)/shard_map/ppermute | solution.py:387
  3.3 13.1 %collective-permute-start.3 = (bf16[256,320]{1,0:T(8,128)(2,1)S(1)}, bf16[256,320]{1,0:T(8,128)(2,1)S(1)}, u32[]{:S(2)}, u32[]{:S(2)}) collective-permute-start(bf16[256,320]{1,0:T(8,128)(2,1)S(1)} %get-tuple-element.22), channel_id=1, source_target_pairs={{1,2},{2,1},{3,4},{4,3},{5,6},{6,5},{7,8},{8,7},{9,10},{10,9},{11,... | collective-permute-start | bytes 491528 | tf_op jit(solution)/shard_map/ppermute | solution.py:399
  6.7 7.6 %copy-start.1 = (f32[320]{0:T(512)S(1)}, f32[320]{0:T(512)}, u32[]{:S(2)}) copy-start(f32[320]{0:T(512)} %param.6) | copy-start | bytes 3844
  6.7 7.6 %copy-start.2 = (f32[320]{0:T(512)S(1)}, f32[320]{0:T(512)}, u32[]{:S(2)}) copy-start(f32[320]{0:T(512)} %param.7) | copy-start | bytes 3844
  6.7 7.6 %copy-start.3 = (f32[320]{0:T(512)S(1)}, f32[320]{0:T(512)}, u32[]{:S(2)}) copy-start(f32[320]{0:T(512)} %param.9) | copy-start | bytes 3844
  6.7 5.0 %collective-permute-start.4 = (f32[40,128]{1,0:T(8,128)S(1)}, f32[40,128]{1,0:T(8,128)S(1)}, u32[]{:S(2)}, u32[]{:S(2)}) collective-permute-start(f32[40,128]{1,0:T(8,128)S(1)} %add.13.after_ref), channel_id=1, source_target_pairs={{0,5},{1,4},{2,7},{3,6},{4,1},{5,0},{6,3},{7,2},{8,13},{9,12},{10,... | collective-permute-start | bytes 61448 | tf_op jit(solution)/shard_map/ppermute | solution.py:387
  11.7 4.7 %collective-permute-start.5 = (f32[40,128]{1,0:T(8,128)S(1)}, f32[40,128]{1,0:T(8,128)S(1)}, u32[]{:S(2)}, u32[]{:S(2)}) collective-permute-start(f32[40,128]{1,0:T(8,128)S(1)} %add.14), channel_id=1, source_target_pairs={{0,8},{1,9},{2,10},{3,11},{4,12},{5,13},{6,14},{7,15},{8,0},{9,1},... | collective-permute-start | bytes 61448 | tf_op jit(solution)/shard_map/ppermute | solution.py:387

commit v7 on v6

--- a/solution.py
+++ b/solution.py
@@ -23,14 +23,26 @@
     lane = iota((128, channels), 0) - offset
     first = lane * per_group
     ch = iota((128, channels), 1)
-    return ((ch >= first) & (ch < first + per_group) & (lane >= 0)).astype(F32)
+    return ((ch >= first) & (ch < first + per_group) & (lane >= 0)).astype(BF16)
 
 
 def group_onehot_t(channels, per_group, offset):
     lane = iota((channels, 128), 1) - offset
     first = lane * per_group
     ch = iota((channels, 128), 0)
-    return ((ch >= first) & (ch < first + per_group) & (lane >= 0)).astype(F32)
+    return ((ch >= first) & (ch < first + per_group) & (lane >= 0)).astype(BF16)
+
+
+def spread(values, onehot):
+    high = values.astype(BF16)
+    left = values - high.astype(F32)
+    middle = left.astype(BF16)
+    low = (left - middle.astype(F32)).astype(BF16)
+    count = values.shape[0]
+    out = jnp.dot(
+        jnp.concatenate([high, middle, low], axis=0), onehot, preferred_element_type=F32
+    )
+    return out[:count] + out[count : 2 * count] + out[2 * count :]
 
 
 def make_stats(rows, cols, channels, tile_rows):
@@ -70,11 +82,9 @@
             (q_ref, 0, 64),
             (q_ref, 1, 96),
         ):
-            term = jnp.dot(
+            term = spread(
                 ref[half * 32 : half * 32 + 32, :],
                 group_onehot_t(channels, per_group, offset),
-                precision=lax.Precision.HIGHEST,
-                preferred_element_type=F32,
             )
             total = term if total is None else total + term
         stats_ref[0:32, :] = total
@@ -227,12 +237,7 @@
         shift = 0.5 * vec[:, wide_c : wide_c + channels]
         bias = vec[:, 2 * wide_c : 2 * wide_c + channels]
         for half in range(2):
-            wide = jnp.dot(
-                both,
-                group_onehot(channels, per_group, 32 * half),
-                precision=lax.Precision.HIGHEST,
-                preferred_element_type=F32,
-            )
+            wide = spread(both, group_onehot(channels, per_group, 32 * half))
             scale = wide[all_rows:] * gain
             offset = shift - wide[:all_rows] * scale
             sc_ref[32 * half : 32 * half + 32, :] = scale[:32]

time: 20.9 us -> 20.5 us (0.981)
  the two profiles are of different devices: /device:TPU:14 before, /device:TPU:12 now
where the time goes in v7:
time: 20.5 us; the launch traced here: 20.4 us
  starting transfers between devices  8 us (39%)
  Pallas kernels  6.56 us (32%)
  waiting for transfers between devices  4.59 us (22%)
  local copies, waits for them, and re-layouts  1.1 us (5%)
    ppermute x4, waiting for transfers between devices, summed(): lax.ppermute(stats, 'wide', [(i, i ^ mask) for i in range(count)])  4.58 us
    pallas_call x1, Pallas kernels, local(): make_main(rows, cols, channels, out_channels, tile_rows, count)  4.16 us
    ppermute x4, starting transfers between devices, summed(): lax.ppermute(stats, 'wide', [(i, i ^ mask) for i in range(count)])  4.13 us
    ppermute x1, starting transfers between devices, local(): halo_b = lax.ppermute(edge_b, 'wide', pairs_b)  3.38 us
    pallas_call x1, Pallas kernels, local(): taps = make_weights(channels, out_channels)(stats, weight)  1.81 us
    unnamed x8, local copies, waits for them, and re-layouts  1.01 us
    pallas_call x1, Pallas kernels, local(): make_stats(rows, cols, channels, tile_rows)(x)  0.53 us
    ppermute x1, starting transfers between devices, local(): halo_a = lax.ppermute(edge_a, 'wide', pairs_a)  0.5 us
  transfers between devices with their start and end apart: 6, of which 3 were waited for; matrix products, arithmetic and copies ran while one was open for 0% of the time, Pallas kernels for 9%

profile of v7, /device:TPU:12, one launch (start us, length us, event | category | flops | bytes accessed | tf_op | source)
XLA Modules:
  0.0 20.4 jit_solution(15441208463596925572)
XLA Ops:
  0.0 0.0 copy-start
  0.0 1.0 %copy-done = bf16[32,16,320]{2,1,0:T(8,128)(2,1)S(1)} copy-done((bf16[32,16,320]{2,1,0:T(8,128)(2,1)S(1)}, bf16[32,16,320]{2,1,0:T(8,128)(2,1)}, u32[]{:S(2)}) %copy-start) | copy-done | bytes 327704
  1.0 0.5 %block_stats.1 = (f32[40,128]{1,0:T(8,128)S(1)}, bf16[256,320]{1,0:T(8,128)(2,1)S(1)}, bf16[256,320]{1,0:T(8,128)(2,1)S(1)}, bf16[512,320]{1,0:T(8,128)(2,1)S(1)}) custom-call(bf16[512,320]{1,0:T(8,128)(2,1)S(1)} %bitcast.2), custom_call_target="tpu_custom_call" | custom-call | tf_op jit(solution)/shard_map/block_stats/pallas_call | solution.py:383
  1.5 0.0 collective-permute-start
  1.5 0.5 %collective-permute-start.1 = (bf16[256,320]{1,0:T(8,128)(2,1)S(1)}, bf16[256,320]{1,0:T(8,128)(2,1)S(1)}, u32[]{:S(2)}, u32[]{:S(2)}) collective-permute-start(bf16[256,320]{1,0:T(8,128)(2,1)S(1)} %get-tuple-element.20), channel_id=1, source_target_pairs={{0,1},{1,0},{2,3},{3,2},{4,5},{5,4},{6,7},{7,6},{8,9},{9,8},{10,11... | collective-permute-start | bytes 491528 | tf_op jit(solution)/shard_map/ppermute | solution.py:388
  2.0 0.7 %collective-permute-done = f32[40,128]{1,0:T(8,128)S(1)} collective-permute-done((f32[40,128]{1,0:T(8,128)S(1)}, f32[40,128]{1,0:T(8,128)S(1)}, u32[]{:S(2)}, u32[]{:S(2)}) %collective-permute-start) | collective-permute-done | bytes 20512 | tf_op jit(solution)/shard_map/ppermute | solution.py:392
  2.7 0.3 %collective-permute-start.2 = (f32[40,128]{1,0:T(8,128)S(1)}, f32[40,128]{1,0:T(8,128)S(1)}, u32[]{:S(2)}, u32[]{:S(2)}) collective-permute-start(f32[40,128]{1,0:T(8,128)S(1)} %add.12.after_ref), channel_id=1, source_target_pairs={{0,3},{1,2},{2,1},{3,0},{4,7},{5,6},{6,5},{7,4},{8,11},{9,10},{10,... | collective-permute-start | bytes 61448 | tf_op jit(solution)/shard_map/ppermute | solution.py:392
  3.0 0.1 blend_weights.1.bw_ref
  3.1 3.4 %collective-permute-start.3 = (bf16[256,320]{1,0:T(8,128)(2,1)S(1)}, bf16[256,320]{1,0:T(8,128)(2,1)S(1)}, u32[]{:S(2)}, u32[]{:S(2)}) collective-permute-start(bf16[256,320]{1,0:T(8,128)(2,1)S(1)} %get-tuple-element.22), channel_id=1, source_target_pairs={{1,2},{2,1},{3,4},{4,3},{5,6},{6,5},{7,8},{8,7},{9,10},{10,9},{11,... | collective-permute-start | bytes 491528 | tf_op jit(solution)/shard_map/ppermute | solution.py:404
  6.4 0.0 collective-permute-done.2
  6.5 0.0 copy-start.1
  6.5 0.0 copy-start.2
  6.5 0.0 copy-start.3
  6.5 0.0 collective-permute-done.1.ha_ref
  6.5 1.3 %collective-permute-start.4 = (f32[40,128]{1,0:T(8,128)S(1)}, f32[40,128]{1,0:T(8,128)S(1)}, u32[]{:S(2)}, u32[]{:S(2)}) collective-permute-start(f32[40,128]{1,0:T(8,128)S(1)} %add.13.after_ref), channel_id=1, source_target_pairs={{0,5},{1,4},{2,7},{3,6},{4,1},{5,0},{6,3},{7,2},{8,13},{9,12},{10,... | collective-permute-start | bytes 61448 | tf_op jit(solution)/shard_map/ppermute | solution.py:392
  7.8 1.8 %conv_weights.1.w_ref = bf16[2880,320]{1,0:T(8,128)(2,1)S(1)} custom-call(f32[40,128]{1,0:T(8,128)S(1)} %add.13.after_ref, bf16[3,3,320,320]{3,2,1,0:T(8,128)(2,1)} %w_hbm.1), custom_call_target="tpu_custom_call" | custom-call | flops 5000000000 | tf_op jit(solution)/shard_map/conv_weights/pallas_call | solution.py:408
  9.6 1.9 %collective-permute-done.4 = f32[40,128]{1,0:T(8,128)S(1)} collective-permute-done((f32[40,128]{1,0:T(8,128)S(1)}, f32[40,128]{1,0:T(8,128)S(1)}, u32[]{:S(2)}, u32[]{:S(2)}) %collective-permute-start.4) | collective-permute-done | bytes 20512 | tf_op jit(solution)/shard_map/ppermute | solution.py:392
  11.5 2.5 %collective-permute-start.5 = (f32[40,128]{1,0:T(8,128)S(1)}, f32[40,128]{1,0:T(8,128)S(1)}, u32[]{:S(2)}, u32[]{:S(2)}) collective-permute-start(f32[40,128]{1,0:T(8,128)S(1)} %add.14), channel_id=1, source_target_pairs={{0,8},{1,9},{2,10},{3,11},{4,12},{5,13},{6,14},{7,15},{8,0},{9,1},... | collective-permute-start | bytes 61448 | tf_op jit(solution)/shard_map/ppermute | solution.py:392
  14.0 0.0 copy-done.1
  14.0 0.0 copy-done.2
  14.0 0.0 copy-done.3
  14.1 0.1 concatenate.3.vec_ref
  14.1 2.0 %collective-permute-done.5 = f32[40,128]{1,0:T(8,128)S(1)} collective-permute-done((f32[40,128]{1,0:T(8,128)S(1)}, f32[40,128]{1,0:T(8,128)S(1)}, u32[]{:S(2)}, u32[]{:S(2)}) %collective-permute-start.5) | collective-permute-done | bytes 20512 | tf_op jit(solution)/shard_map/ppermute | solution.py:392
  16.2 0.0 collective-permute-done.3.hb_ref
  16.2 4.2 %norm_conv.1 = bf16[512,320]{1,0:T(8,128)(2,1)} custom-call(bf16[512,320]{1,0:T(8,128)(2,1)S(1)} %get-tuple-element.16.x_ref, bf16[256,320]{1,0:T(8,128)(2,1)S(1)} %collective-permute-done.1.ha_ref, bf16[256,320]{1,0:T(8,128)(2,1)S(1)} %collective-permute-done.3.hb_ref, f32[40,128]{1,0:T(8,128)S(1)} %add.15.stats_ref, f32[1152]{0:T(1024)S(1)} %concatenate.3.vec_ref, ...), custom_call_target="tpu_custom_call" | custom-call | tf_op jit(solution)/shard_map/norm_conv/pallas_call | solution.py:411
  (5 shorter events, 0.0 us)
Async XLA Ops:
  0.0 1.0 %copy-start = (bf16[32,16,320]{2,1,0:T(8,128)(2,1)S(1)}, bf16[32,16,320]{2,1,0:T(8,128)(2,1)}, u32[]{:S(2)}) copy-start(bf16[32,16,320]{2,1,0:T(8,128)(2,1)} %param.5) | copy-start | bytes 983044
  1.5 1.2 %collective-permute-start = (f32[40,128]{1,0:T(8,128)S(1)}, f32[40,128]{1,0:T(8,128)S(1)}, u32[]{:S(2)}, u32[]{:S(2)}) collective-permute-start(f32[40,128]{1,0:T(8,128)S(1)} %get-tuple-element.18), channel_id=1, source_target_pairs={{0,1},{1,0},{2,3},{3,2},{4,5},{5,4},{6,7},{7,6},{8,9},{9,8},{10,11... | collective-permute-start | bytes 61448 | tf_op jit(solution)/shard_map/ppermute | solution.py:392
  1.5 5.0 %collective-permute-start.1 = (bf16[256,320]{1,0:T(8,128)(2,1)S(1)}, bf16[256,320]{1,0:T(8,128)(2,1)S(1)}, u32[]{:S(2)}, u32[]{:S(2)}) collective-permute-start(bf16[256,320]{1,0:T(8,128)(2,1)S(1)} %get-tuple-element.20), channel_id=1, source_target_pairs={{0,1},{1,0},{2,3},{3,2},{4,5},{5,4},{6,7},{7,6},{8,9},{9,8},{10,11... | collective-permute-start | bytes 491528 | tf_op jit(solution)/shard_map/ppermute | solution.py:388
  2.7 3.7 %collective-permute-start.2 = (f32[40,128]{1,0:T(8,128)S(1)}, f32[40,128]{1,0:T(8,128)S(1)}, u32[]{:S(2)}, u32[]{:S(2)}) collective-permute-start(f32[40,128]{1,0:T(8,128)S(1)} %add.12.after_ref), channel_id=1, source_target_pairs={{0,3},{1,2},{2,1},{3,0},{4,7},{5,6},{6,5},{7,4},{8,11},{9,10},{10,... | collective-permute-start | bytes 61448 | tf_op jit(solution)/shard_map/ppermute | solution.py:392
  3.1 13.1 %collective-permute-start.3 = (bf16[256,320]{1,0:T(8,128)(2,1)S(1)}, bf16[256,320]{1,0:T(8,128)(2,1)S(1)}, u32[]{:S(2)}, u32[]{:S(2)}) collective-permute-start(bf16[256,320]{1,0:T(8,128)(2,1)S(1)} %get-tuple-element.22), channel_id=1, source_target_pairs={{1,2},{2,1},{3,4},{4,3},{5,6},{6,5},{7,8},{8,7},{9,10},{10,9},{11,... | collective-permute-start | bytes 491528 | tf_op jit(solution)/shard_map/ppermute | solution.py:404
  6.5 7.6 %copy-start.1 = (f32[320]{0:T(512)S(1)}, f32[320]{0:T(512)}, u32[]{:S(2)}) copy-start(f32[320]{0:T(512)} %param.6) | copy-start | bytes 3844
  6.5 7.6 %copy-start.2 = (f32[320]{0:T(512)S(1)}, f32[320]{0:T(512)}, u32[]{:S(2)}) copy-start(f32[320]{0:T(512)} %param.7) | copy-start | bytes 3844
  6.5 7.6 %copy-start.3 = (f32[320]{0:T(512)S(1)}, f32[320]{0:T(512)}, u32[]{:S(2)}) copy-start(f32[320]{0:T(512)} %param.9) | copy-start | bytes 3844
  6.5 5.0 %collective-permute-start.4 = (f32[40,128]{1,0:T(8,128)S(1)}, f32[40,128]{1,0:T(8,128)S(1)}, u32[]{:S(2)}, u32[]{:S(2)}) collective-permute-start(f32[40,128]{1,0:T(8,128)S(1)} %add.13.after_ref), channel_id=1, source_target_pairs={{0,5},{1,4},{2,7},{3,6},{4,1},{5,0},{6,3},{7,2},{8,13},{9,12},{10,... | collective-permute-start | bytes 61448 | tf_op jit(solution)/shard_map/ppermute | solution.py:392
  11.5 4.7 %collective-permute-start.5 = (f32[40,128]{1,0:T(8,128)S(1)}, f32[40,128]{1,0:T(8,128)S(1)}, u32[]{:S(2)}, u32[]{:S(2)}) collective-permute-start(f32[40,128]{1,0:T(8,128)S(1)} %add.14), channel_id=1, source_target_pairs={{0,8},{1,9},{2,10},{3,11},{4,12},{5,13},{6,14},{7,15},{8,0},{9,1},... | collective-permute-start | bytes 61448 | tf_op jit(solution)/shard_map/ppermute | solution.py:392

commit v8 on v7

--- a/solution.py
+++ b/solution.py
@@ -120,7 +120,7 @@
         block = lax.axis_index("wide")
         tile0 = lax.div(block + rim // cols, STRIDE // cols)
         tile1 = tile0 - 1
-        sub_id = iota((8, channels), 0)
+        sub_id = iota((8, 128), 0)
         for k in range(3):
             if k < 2:
                 col = sub_id + 8 * k
@@ -147,7 +147,7 @@
         kernel,
         in_specs=[pl.BlockSpec(memory_space=pl.ANY)],
         out_specs=pl.BlockSpec(memory_space=pltpu.VMEM),
-        out_shape=jax.ShapeDtypeStruct((3, 3, 2, 8, channels), F32),
+        out_shape=jax.ShapeDtypeStruct((3, 3, 2, 8, 128), F32),
         compiler_params=pltpu.CompilerParams(vmem_limit_bytes=16 * 2**20),
         cost_estimate=pl.CostEstimate(flops=5000000000, bytes_accessed=0, transcendentals=0),
         name="blend_weights",
@@ -256,6 +256,11 @@
         right_ok = jnp.where(block < count - 1, 1.0, 0.0).astype(F32)
 
         sub_id = iota((8, channels), 0)
+        def weight(j, k, t):
+            w = bw_ref[j, k, t]
+            parts = [w] * (channels // 128) + ([w[:, :rem]] if rem else [])
+            return jnp.concatenate(parts, axis=1)
+
         def silu(x, scale, offset):
             h = x * scale + offset
             return h + h * jnp.tanh(h)
@@ -289,7 +294,7 @@
                 def mix(j, k):
                     if tiles == 1:
                         return acts[k][0] if k < 2 else acts[k][0] * rim_ok
-                    return bw_ref[j, k, 0] * acts[k][0] + bw_ref[j, k, 1] * acts[k][1]
+                    return weight(j, k, 0) * acts[k][0] + weight(j, k, 1) * acts[k][1]
 
                 blend_ref[1, r, 0:8, :] = mix(1, 0)
                 blend_ref[1, r, 8:16, :] = mix(1, 1)

time: 20.5 us -> 20.5 us (level)
  the two profiles are of different devices: /device:TPU:12 before, /device:TPU:14 now
where the time goes in v8:
time: 20.5 us; the launch traced here: 20.3 us
  starting transfers between devices  8 us (39%)
  Pallas kernels  6.52 us (32%)
  waiting for transfers between devices  4.59 us (22%)
  local copies, waits for them, and re-layouts  1.1 us (5%)
    ppermute x4, waiting for transfers between devices, summed(): lax.ppermute(stats, 'wide', [(i, i ^ mask) for i in range(count)])  4.58 us
    pallas_call x1, Pallas kernels, local(): make_main(rows, cols, channels, out_channels, tile_rows, count)  4.13 us
    ppermute x4, starting transfers between devices, summed(): lax.ppermute(stats, 'wide', [(i, i ^ mask) for i in range(count)])  4.12 us
    ppermute x1, starting transfers between devices, local(): halo_b = lax.ppermute(edge_b, 'wide', pairs_b)  3.38 us
    pallas_call x1, Pallas kernels, local(): taps = make_weights(channels, out_channels)(stats, weight)  1.81 us
    unnamed x8, local copies, waits for them, and re-layouts  1.01 us
    pallas_call x1, Pallas kernels, local(): make_stats(rows, cols, channels, tile_rows)(x)  0.53 us
    ppermute x1, starting transfers between devices, local(): halo_a = lax.ppermute(edge_a, 'wide', pairs_a)  0.5 us
  transfers between devices with their start and end apart: 6, of which 3 were waited for; matrix products, arithmetic and copies ran while one was open for 0% of the time, Pallas kernels for 9%

profile of v8, /device:TPU:14, one launch (start us, length us, event | category | flops | bytes accessed | tf_op | source)
XLA Modules:
  0.0 20.3 jit_solution(139632989988904734)
XLA Ops:
  0.0 0.0 copy-start
  0.0 1.0 %copy-done = bf16[32,16,320]{2,1,0:T(8,128)(2,1)S(1)} copy-done((bf16[32,16,320]{2,1,0:T(8,128)(2,1)S(1)}, bf16[32,16,320]{2,1,0:T(8,128)(2,1)}, u32[]{:S(2)}) %copy-start) | copy-done | bytes 327704
  1.0 0.5 %block_stats.1 = (f32[40,128]{1,0:T(8,128)S(1)}, bf16[256,320]{1,0:T(8,128)(2,1)S(1)}, bf16[256,320]{1,0:T(8,128)(2,1)S(1)}, bf16[512,320]{1,0:T(8,128)(2,1)S(1)}) custom-call(bf16[512,320]{1,0:T(8,128)(2,1)S(1)} %bitcast.2), custom_call_target="tpu_custom_call" | custom-call | tf_op jit(solution)/shard_map/block_stats/pallas_call | solution.py:388
  1.5 0.0 collective-permute-start
  1.5 0.5 %collective-permute-start.1 = (bf16[256,320]{1,0:T(8,128)(2,1)S(1)}, bf16[256,320]{1,0:T(8,128)(2,1)S(1)}, u32[]{:S(2)}, u32[]{:S(2)}) collective-permute-start(bf16[256,320]{1,0:T(8,128)(2,1)S(1)} %get-tuple-element.20), channel_id=1, source_target_pairs={{0,1},{1,0},{2,3},{3,2},{4,5},{5,4},{6,7},{7,6},{8,9},{9,8},{10,11... | collective-permute-start | bytes 491528 | tf_op jit(solution)/shard_map/ppermute | solution.py:393
  2.0 0.7 %collective-permute-done = f32[40,128]{1,0:T(8,128)S(1)} collective-permute-done((f32[40,128]{1,0:T(8,128)S(1)}, f32[40,128]{1,0:T(8,128)S(1)}, u32[]{:S(2)}, u32[]{:S(2)}) %collective-permute-start) | collective-permute-done | bytes 20512 | tf_op jit(solution)/shard_map/ppermute | solution.py:397
  2.7 0.3 %collective-permute-start.2 = (f32[40,128]{1,0:T(8,128)S(1)}, f32[40,128]{1,0:T(8,128)S(1)}, u32[]{:S(2)}, u32[]{:S(2)}) collective-permute-start(f32[40,128]{1,0:T(8,128)S(1)} %add.12.after_ref), channel_id=1, source_target_pairs={{0,3},{1,2},{2,1},{3,0},{4,7},{5,6},{6,5},{7,4},{8,11},{9,10},{10,... | collective-permute-start | bytes 61448 | tf_op jit(solution)/shard_map/ppermute | solution.py:397
  3.0 0.1 blend_weights.1.bw_ref
  3.1 3.4 %collective-permute-start.3 = (bf16[256,320]{1,0:T(8,128)(2,1)S(1)}, bf16[256,320]{1,0:T(8,128)(2,1)S(1)}, u32[]{:S(2)}, u32[]{:S(2)}) collective-permute-start(bf16[256,320]{1,0:T(8,128)(2,1)S(1)} %get-tuple-element.22), channel_id=1, source_target_pairs={{1,2},{2,1},{3,4},{4,3},{5,6},{6,5},{7,8},{8,7},{9,10},{10,9},{11,... | collective-permute-start | bytes 491528 | tf_op jit(solution)/shard_map/ppermute | solution.py:409
  6.4 0.0 collective-permute-done.2
  6.5 0.0 copy-start.1
  6.5 0.0 copy-start.2
  6.5 0.0 copy-start.3
  6.5 0.0 collective-permute-done.1.ha_ref
  6.5 1.3 %collective-permute-start.4 = (f32[40,128]{1,0:T(8,128)S(1)}, f32[40,128]{1,0:T(8,128)S(1)}, u32[]{:S(2)}, u32[]{:S(2)}) collective-permute-start(f32[40,128]{1,0:T(8,128)S(1)} %add.13.after_ref), channel_id=1, source_target_pairs={{0,5},{1,4},{2,7},{3,6},{4,1},{5,0},{6,3},{7,2},{8,13},{9,12},{10,... | collective-permute-start | bytes 61448 | tf_op jit(solution)/shard_map/ppermute | solution.py:397
  7.8 1.8 %conv_weights.1.w_ref = bf16[2880,320]{1,0:T(8,128)(2,1)S(1)} custom-call(f32[40,128]{1,0:T(8,128)S(1)} %add.13.after_ref, bf16[3,3,320,320]{3,2,1,0:T(8,128)(2,1)} %w_hbm.1), custom_call_target="tpu_custom_call" | custom-call | flops 5000000000 | tf_op jit(solution)/shard_map/conv_weights/pallas_call | solution.py:413
  9.6 1.9 %collective-permute-done.4 = f32[40,128]{1,0:T(8,128)S(1)} collective-permute-done((f32[40,128]{1,0:T(8,128)S(1)}, f32[40,128]{1,0:T(8,128)S(1)}, u32[]{:S(2)}, u32[]{:S(2)}) %collective-permute-start.4) | collective-permute-done | bytes 20512 | tf_op jit(solution)/shard_map/ppermute | solution.py:397
  11.5 2.5 %collective-permute-start.5 = (f32[40,128]{1,0:T(8,128)S(1)}, f32[40,128]{1,0:T(8,128)S(1)}, u32[]{:S(2)}, u32[]{:S(2)}) collective-permute-start(f32[40,128]{1,0:T(8,128)S(1)} %add.14), channel_id=1, source_target_pairs={{0,8},{1,9},{2,10},{3,11},{4,12},{5,13},{6,14},{7,15},{8,0},{9,1},... | collective-permute-start | bytes 61448 | tf_op jit(solution)/shard_map/ppermute | solution.py:397
  14.0 0.0 copy-done.1
  14.0 0.0 copy-done.2
  14.0 0.0 copy-done.3
  14.0 0.1 concatenate.3.vec_ref
  14.1 2.0 %collective-permute-done.5 = f32[40,128]{1,0:T(8,128)S(1)} collective-permute-done((f32[40,128]{1,0:T(8,128)S(1)}, f32[40,128]{1,0:T(8,128)S(1)}, u32[]{:S(2)}, u32[]{:S(2)}) %collective-permute-start.5) | collective-permute-done | bytes 20512 | tf_op jit(solution)/shard_map/ppermute | solution.py:397
  16.2 0.0 collective-permute-done.3.hb_ref
  16.2 4.1 %norm_conv.1 = bf16[512,320]{1,0:T(8,128)(2,1)} custom-call(bf16[512,320]{1,0:T(8,128)(2,1)S(1)} %get-tuple-element.16.x_ref, bf16[256,320]{1,0:T(8,128)(2,1)S(1)} %collective-permute-done.1.ha_ref, bf16[256,320]{1,0:T(8,128)(2,1)S(1)} %collective-permute-done.3.hb_ref, f32[40,128]{1,0:T(8,128)S(1)} %add.15.stats_ref, f32[1152]{0:T(1024)S(1)} %concatenate.3.vec_ref, ...), custom_call_target="tpu_custom_call" | custom-call | tf_op jit(solution)/shard_map/norm_conv/pallas_call | solution.py:416
  (5 shorter events, 0.0 us)
Async XLA Ops:
  0.0 1.0 %copy-start = (bf16[32,16,320]{2,1,0:T(8,128)(2,1)S(1)}, bf16[32,16,320]{2,1,0:T(8,128)(2,1)}, u32[]{:S(2)}) copy-start(bf16[32,16,320]{2,1,0:T(8,128)(2,1)} %param.5) | copy-start | bytes 983044
  1.5 1.2 %collective-permute-start = (f32[40,128]{1,0:T(8,128)S(1)}, f32[40,128]{1,0:T(8,128)S(1)}, u32[]{:S(2)}, u32[]{:S(2)}) collective-permute-start(f32[40,128]{1,0:T(8,128)S(1)} %get-tuple-element.18), channel_id=1, source_target_pairs={{0,1},{1,0},{2,3},{3,2},{4,5},{5,4},{6,7},{7,6},{8,9},{9,8},{10,11... | collective-permute-start | bytes 61448 | tf_op jit(solution)/shard_map/ppermute | solution.py:397
  1.5 5.0 %collective-permute-start.1 = (bf16[256,320]{1,0:T(8,128)(2,1)S(1)}, bf16[256,320]{1,0:T(8,128)(2,1)S(1)}, u32[]{:S(2)}, u32[]{:S(2)}) collective-permute-start(bf16[256,320]{1,0:T(8,128)(2,1)S(1)} %get-tuple-element.20), channel_id=1, source_target_pairs={{0,1},{1,0},{2,3},{3,2},{4,5},{5,4},{6,7},{7,6},{8,9},{9,8},{10,11... | collective-permute-start | bytes 491528 | tf_op jit(solution)/shard_map/ppermute | solution.py:393
  2.7 3.7 %collective-permute-start.2 = (f32[40,128]{1,0:T(8,128)S(1)}, f32[40,128]{1,0:T(8,128)S(1)}, u32[]{:S(2)}, u32[]{:S(2)}) collective-permute-start(f32[40,128]{1,0:T(8,128)S(1)} %add.12.after_ref), channel_id=1, source_target_pairs={{0,3},{1,2},{2,1},{3,0},{4,7},{5,6},{6,5},{7,4},{8,11},{9,10},{10,... | collective-permute-start | bytes 61448 | tf_op jit(solution)/shard_map/ppermute | solution.py:397
  3.1 13.1 %collective-permute-start.3 = (bf16[256,320]{1,0:T(8,128)(2,1)S(1)}, bf16[256,320]{1,0:T(8,128)(2,1)S(1)}, u32[]{:S(2)}, u32[]{:S(2)}) collective-permute-start(bf16[256,320]{1,0:T(8,128)(2,1)S(1)} %get-tuple-element.22), channel_id=1, source_target_pairs={{1,2},{2,1},{3,4},{4,3},{5,6},{6,5},{7,8},{8,7},{9,10},{10,9},{11,... | collective-permute-start | bytes 491528 | tf_op jit(solution)/shard_map/ppermute | solution.py:409
  6.5 7.6 %copy-start.1 = (f32[320]{0:T(512)S(1)}, f32[320]{0:T(512)}, u32[]{:S(2)}) copy-start(f32[320]{0:T(512)} %param.6) | copy-start | bytes 3844
  6.5 7.6 %copy-start.2 = (f32[320]{0:T(512)S(1)}, f32[320]{0:T(512)}, u32[]{:S(2)}) copy-start(f32[320]{0:T(512)} %param.7) | copy-start | bytes 3844
  6.5 7.6 %copy-start.3 = (f32[320]{0:T(512)S(1)}, f32[320]{0:T(512)}, u32[]{:S(2)}) copy-start(f32[320]{0:T(512)} %param.9) | copy-start | bytes 3844
  6.5 5.0 %collective-permute-start.4 = (f32[40,128]{1,0:T(8,128)S(1)}, f32[40,128]{1,0:T(8,128)S(1)}, u32[]{:S(2)}, u32[]{:S(2)}) collective-permute-start(f32[40,128]{1,0:T(8,128)S(1)} %add.13.after_ref), channel_id=1, source_target_pairs={{0,5},{1,4},{2,7},{3,6},{4,1},{5,0},{6,3},{7,2},{8,13},{9,12},{10,... | collective-permute-start | bytes 61448 | tf_op jit(solution)/shard_map/ppermute | solution.py:397
  11.5 4.7 %collective-permute-start.5 = (f32[40,128]{1,0:T(8,128)S(1)}, f32[40,128]{1,0:T(8,128)S(1)}, u32[]{:S(2)}, u32[]{:S(2)}) collective-permute-start(f32[40,128]{1,0:T(8,128)S(1)} %add.14), channel_id=1, source_target_pairs={{0,8},{1,9},{2,10},{3,11},{4,12},{5,13},{6,14},{7,15},{8,0},{9,1},... | collective-permute-start | bytes 61448 | tf_op jit(solution)/shard_map/ppermute | solution.py:397
